TPU v7x, 32 devices: a whole 2x2x4 slice. The times are simulated.
32 devices in a mesh: dp: 2 (over x), tensor: 8 (over z, y), group: 2 (over core).
Axes of the slice: x: 2, y: 2, z: 4, core: 2. Of those that a mesh axis runs over, the one named last changes fastest.
Arguments:
- resid: bfloat16 [256, 4096], P('dp'), may hold values from -6 to 6
- mixer_out: bfloat16 [256, 8192], P('dp', ('tensor', 'group')), may hold values from -6 to 6
- out_proj: bfloat16 [8192, 4096], P(('tensor', 'group')), may hold values from -0.0625 to 0.0625
- norm_gain: float32 [4096], replicated, may hold values from 0.1 to 1.9
- router: float32 [4096, 4], replicated, may hold values from -0.09375 to 0.09375
- routes: int32 [256, 2], P('dp'), may hold values from 0 to 3, all different within a row; in each aligned block of 128 rows (0 to 127, 128 to 255, ...) at most 96 rows name the same one
- w_gate: bfloat16 [8, 4096, 3584], P('tensor', None, ('dp', 'group')), may hold values from -0.09375 to 0.09375
- w_up: bfloat16 [8, 4096, 3584], P('tensor', None, ('dp', 'group')), may hold values from -0.09375 to 0.09375
- w_down: bfloat16 [8, 3584, 4096], P('tensor', ('dp', 'group')), may hold values from -0.0625 to 0.0625
- cotangent: bfloat16 [256, 4096], P('dp'), may hold values from -6 to 6
Outputs:
- layer_out: bfloat16 [256, 4096], P('dp')
- grad_mixer: bfloat16 [256, 8192], P('dp', ('tensor', 'group'))
- grad_down: bfloat16 [8, 3584, 4096], P('tensor', ('dp', 'group'))
Inputs may be any that keep to these rules, and one draw needn't show every extreme that they name: `routes`: in each aligned block of 128 rows (the tokens of one replica) no expert is named by more than 96 rows, and some expert reaches 96 in some block; the two experts of a row differ.
All inputs are finite; a program needn't handle non-finite values.
Results may differ from a plain program's by a relative error of at most 0.03.
Values may be sent and summed in bfloat16 or wider, within the bound.
A program may use at most 128 MiB of HBM per device.

v0:
```python
import jax
import jax.numpy as jnp
from jax import lax
from jax.sharding import PartitionSpec as P


def contract_rows(left, right):
    return lax.dot_general(
        left, right, (((0,), (0,)), ((), ())), preferred_element_type=jnp.float32
    )


def contract_cols(left, right):
    return lax.dot_general(
        left, right, (((1,), (1,)), ((), ())), preferred_element_type=jnp.float32
    )


def norm_forward(hidden, norm_gain):
    inv_rms = lax.rsqrt(jnp.mean(hidden * hidden, axis=1, keepdims=True) + 1e-05)
    return ((hidden * inv_rms * norm_gain).astype(jnp.bfloat16), inv_rms)


def norm_backward(hidden, inv_rms, norm_gain, normed_cot):
    weighted = normed_cot * norm_gain
    inner_mean = jnp.mean(weighted * hidden, axis=1, keepdims=True)
    return inv_rms * weighted - inv_rms * inv_rms * inv_rms * hidden * inner_mean


def pair_slots(pair_expert, expert_count):
    onehot = (pair_expert[:, None] == jnp.arange(expert_count, dtype=jnp.int32)[None, :]).astype(
        jnp.int32
    )
    before = jnp.cumsum(onehot, axis=0) - onehot
    return (jnp.sum(before * onehot, axis=1), onehot)


def join_experts(half_sums, capacity, expert_count):
    model_width = half_sums.shape[1]
    half_out = half_sums.astype(jnp.bfloat16)
    gathered = lax.all_gather(half_out, ("tensor", "group"), axis=0, tiled=True)
    gathered = gathered.reshape(expert_count, 2, capacity, model_width).astype(jnp.float32)
    return (
        (gathered[:, 0] + gathered[:, 1])
        .astype(jnp.bfloat16)
        .reshape(expert_count * capacity, model_width)
    )


def on_device(
    resid, mixer_out, out_proj, norm_gain, router, routes, w_gate, w_up, w_down, cotangent
):
    row_count = resid.shape[0]
    model_width = resid.shape[1]
    expert_count = router.shape[1]
    units_here = w_gate.shape[2]
    capacity = min(row_count, 3 * row_count // expert_count)
    expert_id = lax.axis_index("tensor") // 2
    own_term = jnp.dot(mixer_out, out_proj, preferred_element_type=jnp.float32)
    summed = lax.psum(own_term.astype(jnp.bfloat16), ("tensor", "group")).astype(jnp.float32)
    hidden = resid.astype(jnp.float32) + summed
    normed, inv_rms = norm_forward(hidden, norm_gain)
    logits = jnp.dot(normed.astype(jnp.float32), router, precision=lax.Precision.HIGHEST)
    pair_expert = routes.reshape(-1)
    slot_pos, onehot = pair_slots(pair_expert, expert_count)
    onehot_f = onehot.astype(jnp.float32)
    target = pair_expert * capacity + slot_pos
    pair_select = (
        target[:, None] == jnp.arange(expert_count * capacity, dtype=jnp.int32)[None, :]
    ).astype(jnp.bfloat16)
    own_select = lax.dynamic_slice_in_dim(pair_select, expert_id * capacity, capacity, 1)
    pair_logit = jnp.sum(jnp.repeat(logits, 2, axis=0) * onehot_f, axis=1)
    gate_vals = jax.nn.sigmoid(pair_logit)
    pair_rows = jnp.repeat(normed, 2, axis=0)
    local_rows = contract_rows(own_select, pair_rows).astype(jnp.bfloat16)
    cot_full = cotangent.astype(jnp.float32)
    pair_cot = jnp.repeat(cot_full, 2, axis=0)
    out_cot = (gate_vals[:, None] * pair_cot).astype(jnp.bfloat16)
    local_cots = contract_rows(own_select, out_cot).astype(jnp.bfloat16)
    gate_up = jnp.concatenate((w_gate[0], w_up[0]), axis=1)
    pre_both = jnp.dot(
        lax.all_gather(local_rows, "dp", axis=0, tiled=True),
        gate_up,
        preferred_element_type=jnp.float32,
    )
    pre_gate = pre_both[:, :units_here]
    pre_up = pre_both[:, units_here:]
    sig_gate = jax.nn.sigmoid(pre_gate)
    activated = (pre_gate * sig_gate * pre_up).astype(jnp.bfloat16)
    own_out = lax.psum_scatter(
        jnp.dot(activated, w_down[0], preferred_element_type=jnp.float32).astype(jnp.bfloat16),
        ("dp", "group"),
        scatter_dimension=0,
        tiled=True,
    ).astype(jnp.float32)
    returned = join_experts(own_out, capacity, expert_count)
    pair_out = jnp.dot(pair_select, returned, preferred_element_type=jnp.float32)
    mixture = jnp.sum((gate_vals[:, None] * pair_out).reshape(row_count, 2, model_width), axis=1)
    layer_out = (hidden + mixture).astype(jnp.bfloat16)
    gate_cot = jnp.sum(pair_cot * pair_out, axis=1)
    slot_cot = lax.all_gather(local_cots, "dp", axis=0, tiled=True)
    act_cot = contract_cols(slot_cot, w_down[0])
    d_gate = (act_cot * pre_up * sig_gate * (1.0 + pre_gate * (1.0 - sig_gate))).astype(
        jnp.bfloat16
    )
    d_up = (act_cot * pre_gate * sig_gate).astype(jnp.bfloat16)
    own_in = lax.psum_scatter(
        (contract_cols(d_gate, w_gate[0]) + contract_cols(d_up, w_up[0])).astype(jnp.bfloat16),
        ("dp", "group"),
        scatter_dimension=0,
        tiled=True,
    ).astype(jnp.float32)
    returned_cot = join_experts(own_in, capacity, expert_count)
    grad_down = contract_rows(activated, slot_cot).astype(jnp.bfloat16)[None]
    pair_in = jnp.dot(pair_select, returned_cot, preferred_element_type=jnp.float32)
    normed_cot = jnp.sum(pair_in.reshape(row_count, 2, model_width), axis=1)
    logit_pair = gate_cot * gate_vals * (1.0 - gate_vals)
    logit_cot = jnp.sum(
        (onehot_f * logit_pair[:, None]).reshape(row_count, 2, expert_count), axis=1
    )
    normed_cot = normed_cot + jnp.dot(logit_cot, router.T, precision=lax.Precision.HIGHEST)
    hidden_cot = (cot_full + norm_backward(hidden, inv_rms, norm_gain, normed_cot)).astype(
        jnp.bfloat16
    )
    grad_mixer = contract_cols(hidden_cot, out_proj).astype(jnp.bfloat16)
    return (layer_out, grad_mixer, grad_down)


def solution(mesh):
    placed = (
        P("dp", None),
        P("dp", ("tensor", "group")),
        P(("tensor", "group"), None),
        P(),
        P(),
        P("dp", None),
        P("tensor", None, ("dp", "group")),
        P("tensor", None, ("dp", "group")),
        P("tensor", ("dp", "group"), None),
        P("dp", None),
    )
    return jax.shard_map(
        on_device,
        mesh=mesh,
        in_specs=placed,
        out_specs=(P("dp", None), P("dp", ("tensor", "group")), P("tensor", ("dp", "group"), None)),
        check_vma=False,
    )
```

profile of v0, /device:TPU:0, one launch (start us, length us, event | category | flops | bytes accessed | tf_op | source)
XLA Modules:
  0.0 430.3 jit_solution(9105785876515630583)
XLA Ops:
  8.1 3.9 convolution_convert_fusion
  14.3 93.9 %all-reduce.2.cloned.1.call-done = bf16[128,4096]{1,0:T(8,128)(2,1)} async-done(((bf16[128,4096]{1,0:T(8,128)(2,1)}), bf16[128,4096]{1,0:T(8,128)(2,1)}) %all-reduce.2.cloned.1.call-update) | async-done | bytes 1048592 | tf_op jit(solution)/shard_map/psum | solution.py:60
  108.1 1.6 multiply_reduce_fusion.2
  110.3 1.6 multiply_convert_fusion.2
  111.9 3.4 broadcast_in_dim.9
  115.4 4.1 reshape.152
  119.5 3.1 convolution_convert_fusion.2
  122.6 26.6 %all-gather.5.cloned.1.call-done = bf16[192,4096]{1,0:T(8,128)(2,1)} async-done(((bf16[96,4096]{1,0:T(8,128)(2,1)}), bf16[192,4096]{1,0:T(8,128)(2,1)}) %all-gather.5.cloned.1.call-update) | async-done | bytes 1572880 | tf_op jit(solution)/shard_map/all_gather | solution.py:82
  149.2 8.7 %fusion = f32[192,1792]{1,0:T(8,128)S(1)} fusion(bf16[192,4096]{1,0:T(8,128)(2,1)} %all-gather.5.cloned.1.call-done, bf16[4096,896]{1,0:T(8,128)(2,1)} %bitcast.62, bf16[4096,896]{1,0:T(8,128)(2,1)} %bitcast.68), kind=kOutput, calls=%fused_computation | convolution fusion | flops 2847932416 | bytes 17629184 | tf_op jit(solution)/shard_map/dot_general | solution.py:81
  159.9 6.1 %fusion.11 = bf16[192,4096]{1,0:T(8,128)(2,1)} fusion(bf16[192,896]{1,0:T(8,128)(2,1)S(1)} %multiply_convert_fusion.5, bf16[1,896,4096]{2,1,0:T(8,128)(2,1)} %param.18), kind=kOutput, calls=%fused_computation.15 | convolution fusion | flops 1410072576 | bytes 9256960 | tf_op jit(solution)/shard_map/dot_general | solution.py:91
  166.1 28.3 %reduce-scatter.3.cloned.1.call-done = bf16[48,4096]{1,0:T(8,128)(2,1)} async-done(((bf16[192,4096]{1,0:T(8,128)(2,1)}), bf16[48,4096]{1,0:T(8,128)(2,1)}) %reduce-scatter.3.cloned.1.call-update) | async-done | bytes 393232 | tf_op jit(solution)/shard_map/reduce_scatter | solution.py:90
  194.6 5.4 %broadcast_in_dim.10 = f32[128,2,4096]{2,1,0:T(2,128)} broadcast(bf16[128,4096]{1,0:T(8,128)(2,1)} %param.19), dimensions={0,2} | broadcast | bytes 5242880 | tf_op jit(solution)/shard_map/broadcast_in_dim | solution.py:77
  200.0 6.1 %reshape.154 = f32[256,4096]{1,0:T(8,128)} reshape(f32[128,2,4096]{2,1,0:T(2,128)} %broadcast_in_dim.10) | data formatting | bytes 8388608 | tf_op jit(solution)/shard_map/reshape | solution.py:77
  207.1 51.6 %all-gather.7.cloned.1.call-done = bf16[768,4096]{1,0:T(8,128)(2,1)} async-done(((bf16[48,4096]{1,0:T(8,128)(2,1)}), bf16[768,4096]{1,0:T(8,128)(2,1)}) %all-gather.7.cloned.1.call-update) | async-done | bytes 6291472 | tf_op jit(solution)/shard_map/all_gather | solution.py:41
  258.6 4.5 %convert.2 = f32[4,2,96,4096]{3,2,1,0:T(8,128)S(1)} convert(bf16[4,2,96,4096]{3,2,1,0:T(8,128)(2,1)} %bitcast.66) | non-fusion elementwise | flops 3145728 | bytes 18874368 | tf_op jit(solution)/shard_map/convert_element_type | solution.py:42
  263.2 2.5 fusion.9
  266.4 5.3 %multiply_reduce_fusion = (f32[256]{0:T(256)S(1)}, f32[256,4096]{1,0:T(8,128)}) fusion(f32[256,4096]{1,0:T(8,128)S(1)} %copy-done.2, bf16[384,4096]{1,0:T(8,128)(2,1)} %bitcast.61, s32[256]{0:T(256)S(1)} %multiply_add_fusion.1), kind=kOutput, calls=%fused_computation.21 | convolution fusion | flops 807501568 | bytes 11536384 | tf_op jit(solution)/shard_map/dot_general | solution.py:97
  272.2 3.7 convolution_convert_fusion.1
  276.0 25.9 %all-gather.9.cloned.1.call-done = bf16[192,4096]{1,0:T(8,128)(2,1)} async-done(((bf16[96,4096]{1,0:T(8,128)(2,1)}), bf16[192,4096]{1,0:T(8,128)(2,1)}) %all-gather.9.cloned.1.call-update) | async-done | bytes 1572880 | tf_op jit(solution)/shard_map/all_gather | solution.py:101
  301.9 6.3 %fusion.4 = f32[192,896]{1,0:T(8,128)S(1)} fusion(bf16[192,4096]{1,0:T(8,128)(2,1)} %all-gather.9.cloned.1.call-done, bf16[1,896,4096]{2,1,0:T(8,128)(2,1)} %param.18), kind=kOutput, calls=%fused_computation.4 | convolution fusion | flops 1409286144 | bytes 9601024 | tf_op jit(solution)/shard_map/dot_general | solution.py:14
  308.2 5.9 %fusion.22 = f32[192,4096]{1,0:T(8,128)S(1)} fusion(f32[192,896]{1,0:T(8,128)S(1)} %fusion.4, f32[192,1792]{1,0:T(8,128)S(1)} %copy-done.9, bf16[1,4096,896]{2,1,0:T(8,128)(2,1)} %param.16), kind=kOutput, calls=%fused_computation.44 | convolution fusion | flops 1411006464 | bytes 12550144 | tf_op jit(solution)/shard_map/dot_general | solution.py:14
  314.1 3.8 fusion.10
  317.9 28.3 %reduce-scatter.5.cloned.1.call-done = bf16[48,4096]{1,0:T(8,128)(2,1)} async-done(((bf16[192,4096]{1,0:T(8,128)(2,1)}), bf16[48,4096]{1,0:T(8,128)(2,1)}) %reduce-scatter.5.cloned.1.call-update) | async-done | bytes 393232 | tf_op jit(solution)/shard_map/reduce_scatter | solution.py:107
  346.5 4.8 %broadcast_multiply_fusion = f32[256,4096]{1,0:T(8,128)} fusion(f32[256,4096]{1,0:T(8,128)} %get-tuple-element.10, f32[256]{0:T(256)S(1)} %div.32), kind=kLoop, calls=%fused_computation.27 | loop fusion | flops 1048576 | bytes 8389632 | tf_op jit(solution)/shard_map/mul | solution.py:98
  351.3 5.8 %reshape.153 = f32[128,2,4096]{2,1,0:T(2,128)} reshape(f32[256,4096]{1,0:T(8,128)} %broadcast_multiply_fusion) | data formatting | bytes 8388608 | tf_op jit(solution)/shard_map/reshape | solution.py:98
  357.1 8.8 %reduce_sum.79 = f32[128,4096]{1,0:T(8,128)} reduce(f32[128,2,4096]{2,1,0:T(2,128)} %reshape.153, f32[]{:T(128)} %constant.31.clone.1), dimensions={1}, to_apply=%region_7.8 | reduce | flops 524288 | bytes 6291460 | tf_op jit(solution)/shard_map/reduce_sum | solution.py:98
  365.9 6.6 %convert_bitcast_fusion = bf16[1,896,4096]{2,1,0:T(8,128)(2,1)} fusion(bf16[192,896]{1,0:T(8,128)(2,1)S(1)} %copy-done.11, bf16[192,4096]{1,0:T(8,128)(2,1)} %all-gather.9.cloned.1.call-done), kind=kOutput, calls=%fused_computation.8 | convolution fusion | flops 1412956160 | bytes 9256960 | tf_op jit(solution)/shard_map/dot_general | solution.py:8
  372.5 37.9 %all-gather.11.cloned.1.call-done = bf16[768,4096]{1,0:T(8,128)(2,1)} async-done(((bf16[48,4096]{1,0:T(8,128)(2,1)}), bf16[768,4096]{1,0:T(8,128)(2,1)}) %all-gather.11.cloned.1.call-update) | async-done | bytes 6291472 | tf_op jit(solution)/shard_map/all_gather | solution.py:41
  410.4 4.5 %convert.3 = f32[4,2,96,4096]{3,2,1,0:T(8,128)S(1)} convert(bf16[4,2,96,4096]{3,2,1,0:T(8,128)(2,1)} %bitcast.65) | non-fusion elementwise | flops 3145728 | bytes 18874368 | tf_op jit(solution)/shard_map/convert_element_type | solution.py:42
  415.8 1.3 convolution_reduce_fusion
  417.7 3.4 multiply_reduce_fusion.1
  421.1 2.3 convolution_convert_fusion.3
  (80 shorter events, 9.9 us)
Async XLA Ops:
  7.2 0.9 copy-start
  7.2 4.9 %copy-start.14 = (s32[128,2]{0,1:T(2,128)S(1)}, s32[128,2]{0,1:T(2,128)}, u32[]{:S(2)}) copy-start(s32[128,2]{0,1:T(2,128)} %param.15) | copy-start | bytes 3076
  7.2 100.9 %copy-start.4 = (bf16[128,4096]{1,0:T(8,128)(2,1)S(1)}, bf16[128,4096]{1,0:T(8,128)(2,1)}, u32[]{:S(2)}) copy-start(bf16[128,4096]{1,0:T(8,128)(2,1)} %param.10) | copy-start | bytes 3145732
  7.2 103.1 %copy-start.13 = (f32[4096]{0:T(1024)S(1)}, f32[4096]{0:T(1024)}, u32[]{:S(2)}) copy-start(f32[4096]{0:T(1024)} %param.13) | copy-start | bytes 49156
  7.2 100.9 %all-reduce.2.cloned.1.call-start = ((), (), s32[]{:S(2)}) async-start(), calls=%async_computation.2 | async-start | bytes 2097152 | tf_op jit(solution)/shard_map/psum | solution.py:60
  12.0 137.2 %all-gather.5.cloned.1.call-start = ((), (), s32[]{:S(2)}) async-start(), calls=%async_computation.3 | async-start | bytes 2359296 | tf_op jit(solution)/shard_map/all_gather | solution.py:82
  122.6 71.8 %reduce-scatter.3.cloned.1.call-start = ((), (), s32[]{:S(2)}) async-start(), calls=%async_computation.4 | async-start | bytes 1966080 | tf_op jit(solution)/shard_map/reduce_scatter | solution.py:90
  157.8 1.1 copy-start.8
  159.1 0.7 copy-start.10
  166.0 92.6 %all-gather.7.cloned.1.call-start = ((), (), s32[]{:S(2)}) async-start(), calls=%async_computation.5 | async-start | bytes 6684672 | tf_op jit(solution)/shard_map/all_gather | solution.py:41
  194.4 107.5 %all-gather.9.cloned.1.call-start = ((), (), s32[]{:S(2)}) async-start(), calls=%async_computation.6 | async-start | bytes 2359296 | tf_op jit(solution)/shard_map/all_gather | solution.py:101
  200.0 6.1 %copy-start.12 = (f32[4096,4]{0,1:T(4,128)S(1)}, f32[4096,4]{0,1:T(4,128)}, u32[]{:S(2)}) copy-start(f32[4096,4]{0,1:T(4,128)} %param.14) | copy-start | bytes 196612
  263.2 3.2 copy-start.2
  275.9 32.2 %copy-start.9 = (f32[192,1792]{1,0:T(8,128)S(1)}, f32[192,1792]{1,0:T(8,128)}, u32[]{:S(2)}) copy-start(f32[192,1792]{1,0:T(8,128)} %copy-done.8) | copy-start | bytes 4128772
  275.9 70.3 %reduce-scatter.5.cloned.1.call-start = ((), (), s32[]{:S(2)}) async-start(), calls=%async_computation.7 | async-start | bytes 1966080 | tf_op jit(solution)/shard_map/reduce_scatter | solution.py:107
  301.9 12.2 %slice-start = ((s8[7340032]{0:T(1024)(128)(4,1)}), s8[4194304]{0:T(1024)(128)(4,1)S(1)}, s32[]{:S(2)}) async-start(s8[7340032]{0:T(1024)(128)(4,1)} %bitcast.63), calls=%async_computation.9 | async-start | bytes 8388608
  308.1 5.9 %slice-start.1 = ((s8[7340032]{0:T(1024)(128)(4,1)}), s8[3145728]{0:T(1024)(128)(4,1)S(1)}, s32[]{:S(2)}) async-start(s8[7340032]{0:T(1024)(128)(4,1)} %bitcast.63), calls=%async_computation.10 | async-start | bytes 6291456
  317.9 92.5 %all-gather.11.cloned.1.call-start = ((), (), s32[]{:S(2)}) async-start(), calls=%async_computation.8 | async-start | bytes 6684672 | tf_op jit(solution)/shard_map/all_gather | solution.py:41
  357.1 8.9 %copy-start.11 = (bf16[192,896]{1,0:T(8,128)(2,1)S(1)}, bf16[192,896]{1,0:T(8,128)(2,1)}, u32[]{:S(2)}) copy-start(bf16[192,896]{1,0:T(8,128)(2,1)} %copy-done.10) | copy-start | bytes 1032196
  415.7 1.3 copy-start.5
  415.8 1.9 copy-start.6
  417.7 3.4 copy-start.3
  417.7 3.4 copy-start.7
  417.7 3.4 copy-start.15
  421.1 2.3 copy-start.1
Sparse Core Ops, SparseCore 0:
  12.1 95.9 all-reduce.1
  122.7 26.4 all-gather.4
  166.1 28.1 reduce-scatter.2
  196.8 61.8 all-gather.6
  276.0 25.7 all-gather.8
  318.0 28.1 reduce-scatter.4
  348.5 61.8 all-gather.10
where the time goes:
time: 431 us; the launch traced here: 430 us
  waiting for transfers between devices  292 us (68%)
  matrix products  61.2 us (14%)
  other arithmetic  31.6 us (7%)
  local copies, waits for them, and re-layouts  30.2 us (7%)
  between operations  14.4 us (3%)
    psum x1, waiting for transfers between devices, on_device(): lax.psum(own_term.astype(jnp.bfloat16), ('tensor', 'group'))  93.9 us
    all_gather x2, waiting for transfers between devices, join_experts(): gathered = lax.all_gather(half_out, ('tensor', 'group'), axis=0, tiled=True)  89.5 us
    reduce_scatter x1, waiting for transfers between devices, on_device(): lax.psum_scatter(jnp.dot(activated, w_down[0], preferred_element_type=jnp...  28.3 us
    reduce_scatter x1, waiting for transfers between devices, on_device(): lax.psum_scatter((contract_cols(d_gate, w_gate[0]) + contract_cols(d_up,...  28.3 us
    all_gather x1, waiting for transfers between devices, on_device(): lax.all_gather(local_rows, 'dp', axis=0, tiled=True)  26.6 us
    all_gather x1, waiting for transfers between devices, on_device(): slot_cot = lax.all_gather(local_cots, 'dp', axis=0, tiled=True)  25.9 us
    dot_general x4, matrix products, contract_cols(): lax.dot_general(left, right, (((1,), (1,)), ((), ())), preferred_element_...  18.2 us
    dot_general x3, matrix products, contract_rows(): lax.dot_general(left, right, (((0,), (0,)), ((), ())), preferred_element_...  13.3 us
  transfers between devices with their start and end apart: 7, of which 7 were waited for; matrix products, arithmetic and copies ran while one was open for 9% of the time, Pallas kernels for 0%

commit v1 on v0

v1 whole, which is shorter than its diff:
```python
import functools

import jax
import jax.numpy as jnp
from jax import lax
from jax.experimental import pallas as pl
from jax.experimental.pallas import tpu as pltpu
from jax.sharding import PartitionSpec as P

MESH = pl.DeviceIdType.MESH
F32 = jnp.float32
BF16 = jnp.bfloat16
VMEM_MIB = 56


def contract_rows(left, right):
    return lax.dot_general(left, right, (((0,), (0,)), ((), ())), preferred_element_type=F32)


def contract_cols(left, right):
    return lax.dot_general(left, right, (((1,), (1,)), ((), ())), preferred_element_type=F32)


def norm_backward(hidden, inv_rms, norm_gain, normed_cot):
    weighted = normed_cot * norm_gain
    inner_mean = jnp.mean(weighted * hidden, axis=1, keepdims=True)
    return inv_rms * weighted - inv_rms * inv_rms * inv_rms * hidden * inner_mean


class Place:
    def __init__(self, n_dp, experts, width):
        self.n_dp, self.experts = n_dp, experts
        self.half, self.quarter, self.piece = width // 2, width // 4, width // (4 * experts)
        self.x, self.c = lax.axis_index("dp"), lax.axis_index("group")
        tensor = lax.axis_index("tensor")
        self.e, self.h = tensor // 2, lax.rem(tensor, 2)

    def device(self, x=None, e=None, h=None, c=None):
        x = self.x if x is None else x
        e = self.e if e is None else e
        h = self.h if h is None else h
        c = self.c if c is None else c
        return (x, 2 * e + h, c)

    def step_x(self, d):
        return lax.rem(self.x + (d + self.n_dp), self.n_dp)

    def step_e(self, d):
        return lax.rem(self.e + (d + self.experts), self.experts)

    def cols_c(self, c):
        return pl.ds(pl.multiple_of(c * self.half, self.half), self.half)

    def cols_h(self, h, c):
        return pl.ds(pl.multiple_of(c * self.half + h * self.quarter, self.quarter), self.quarter)

    def cols_e(self, e, h, c):
        start = c * self.half + h * self.quarter + e * self.piece
        return pl.ds(pl.multiple_of(start, self.piece), self.piece)


class Sender:
    def __init__(self, send_sems, recv_sems):
        self.send_sems, self.recv_sems, self.copies = send_sems, recv_sems, []

    def start(self, src, dst, device):
        k = len(self.copies)
        copy = pltpu.make_async_remote_copy(
            src_ref=src,
            dst_ref=dst,
            send_sem=self.send_sems.at[k],
            recv_sem=self.recv_sems.at[k],
            device_id=device,
            device_id_type=MESH,
        )
        copy.start()
        self.copies.append(copy)
        return copy

    def finish(self):
        for copy in self.copies:
            copy.wait_send()


def greet(devices):
    barrier = pltpu.get_barrier_semaphore()
    for device in devices:
        pl.semaphore_signal(barrier, inc=1, device_id=device, device_id_type=MESH)
    pl.semaphore_wait(barrier, len(devices))


def forward(place, sender, ref, where, **to):
    return sender.start(ref.at[where], ref.at[where], place.device(**to))


def gather_start(place, sender, out):
    here = place
    where = (slice(None), here.cols_e(here.e, here.h, here.c))
    return [None] + [
        forward(here, sender, out, where, e=here.step_e(d)) for d in range(1, here.experts)
    ]


def gather_rest(place, sender, started):
    here = place
    over_h, over_c = {}, []
    for d in range(here.experts):
        where = (slice(None), here.cols_e(here.step_e(-d), here.h, here.c))
        for i, (out, over_e) in enumerate(started):
            if d:
                over_e[d].wait_recv()
            over_h[i, d] = forward(here, sender, out, where, h=1 - here.h)
            over_c.append(forward(here, sender, out, where, c=1 - here.c))
    for d in range(here.experts):
        where = (slice(None), here.cols_e(here.step_e(-d), 1 - here.h, here.c))
        for i, (out, over_e) in enumerate(started):
            over_h[i, d].wait_recv()
            over_c.append(forward(here, sender, out, where, c=1 - here.c))
    for copy in over_c:
        copy.wait_recv()


def gather_and_dispatch(place, sender, over_e, hidden, select_t, rows, rows_of):
    here = place
    steps_x = range(1, here.n_dp)

    def pick(cols):
        rows[rows_of(here.x), cols] = jnp.dot(
            select_t[...], hidden[:, cols], preferred_element_type=F32
        ).astype(BF16)

    over_h, over_c, over_x, rows_h, rows_c = {}, [], {}, {}, []
    for d in range(here.experts):
        cols = here.cols_e(here.step_e(-d), here.h, here.c)
        if d:
            over_e[d].wait_recv()
        over_h[d] = forward(here, sender, hidden, (slice(None), cols), h=1 - here.h)
        over_c.append(forward(here, sender, hidden, (slice(None), cols), c=1 - here.c))
        pick(cols)
        for s in steps_x:
            over_x[d, s] = forward(
                here, sender, rows, (rows_of(here.x), cols), x=here.step_x(s)
            )
    for d in range(here.experts):
        cols = here.cols_e(here.step_e(-d), here.h, here.c)
        for s in steps_x:
            over_x[d, s].wait_recv()
            where = (rows_of(here.step_x(-s)), cols)
            rows_h[d, s] = forward(here, sender, rows, where, h=1 - here.h)
            rows_c.append(forward(here, sender, rows, where, c=1 - here.c))
        other = here.cols_e(here.step_e(-d), 1 - here.h, here.c)
        over_h[d].wait_recv()
        over_c.append(forward(here, sender, hidden, (slice(None), other), c=1 - here.c))
        pick(other)
    for d in range(here.experts):
        cols = here.cols_e(here.step_e(-d), 1 - here.h, here.c)
        for s in steps_x:
            rows_h[d, s].wait_recv()
            where = (rows_of(here.step_x(-s)), cols)
            rows_c.append(forward(here, sender, rows, where, c=1 - here.c))
    for copy in over_c:
        copy.wait_recv()
    pick(here.cols_c(1 - here.c))
    for copy in rows_c:
        copy.wait_recv()


def tiles(extent, most):
    size = 128
    while size * 2 <= most and extent % (size * 2) == 0:
        size *= 2
    return size, extent // size


def layer_kernel(
    n_dp,
    experts,
    own_ref,
    cots_ref,
    select_ref,
    select_t,
    resid_ref,
    gain_ref,
    router_ref,
    gate_hbm,
    up_hbm,
    down_hbm,
    hidden_ref,
    mix_ref,
    cot_ref,
    act_ref,
    out_cot_ref,
    w_gate,
    w_up,
    w_down,
    slot_cot,
    rows,
    own_out,
    own_in,
    swap_in,
    swapped,
    hidden_parts,
    pair_in,
    paired,
    parts,
    tokens,
    pieces,
    d_gate,
    d_up,
    raw_cot,
    pre_gate,
    pre_up,
    gates,
    slopes,
    load_sems,
    send_sems,
    recv_sems,
):
    width = own_ref.shape[1]
    capacity = cots_ref.shape[0]
    slots = n_dp * capacity
    here = Place(n_dp, experts, width)
    sender = Sender(send_sems, recv_sems)
    tensor = 2 * experts
    mine = 2 * here.e + here.h

    def rows_of(x):
        return pl.ds(pl.multiple_of(x * capacity, capacity), capacity)

    loads = [
        pltpu.make_async_copy(src, dst, load_sems.at[k])
        for k, (src, dst) in enumerate(((down_hbm, w_down), (gate_hbm, w_gate), (up_hbm, w_up)))
    ]
    for load in loads:
        load.start()

    peers = []
    for d in range(1, tensor):
        other = lax.rem(mine + d, tensor)
        peers.append((other // 2, lax.rem(other, 2)))
    plane = [(d, flip) for flip in (1, 0) for d in range(n_dp)]
    devices = [here.device(c=1 - here.c)]
    devices += [here.device(e=e, h=h) for e, h in peers]
    devices += [
        here.device(x=here.step_x(d), h=lax.rem(here.h + flip, 2)) for d, flip in plane if d
    ]
    greet(devices)

    swap = sender.start(own_ref.at[:, here.cols_c(1 - here.c)], swap_in, here.device(c=1 - here.c))
    half_cols = here.cols_c(here.c)
    replicas = [
        sender.start(
            cots_ref.at[:, half_cols],
            slot_cot.at[rows_of(here.x), half_cols],
            here.device(x=here.step_x(d)),
        )
        for d in range(1, n_dp)
    ]
    swap.wait_recv()
    swapped[...] = (own_ref[:, half_cols].astype(F32) + swap_in[...].astype(F32)).astype(BF16)
    arrivals = [
        sender.start(swapped.at[:, here.cols_e(e, h, 0)], hidden_parts.at[d], here.device(e=e, h=h))
        for d, (e, h) in enumerate(peers)
    ]
    slot_cot[rows_of(here.x), :] = cots_ref[...]
    shared = []
    for d in range(1, n_dp):
        replicas[d - 1].wait_recv()
        where = (rows_of(here.step_x(-d)), half_cols)
        shared.append(forward(here, sender, slot_cot, where, c=1 - here.c))
    own_cols = here.cols_e(here.e, here.h, here.c)
    total = swapped[:, here.cols_e(here.e, here.h, 0)].astype(F32)
    total = total + resid_ref[:, own_cols].astype(F32)
    for d, copy in enumerate(arrivals):
        copy.wait_recv()
        total = total + hidden_parts[d].astype(F32)
    hidden_ref[:, own_cols] = total.astype(BF16)
    over_e = gather_start(here, sender, hidden_ref)

    for copy in shared:
        copy.wait_recv()
    loads[0].wait()
    depth, steps = tiles(width, 1024)
    raw_cot[...] = jnp.zeros_like(raw_cot)

    @pl.loop(0, steps)
    def _(k):
        cols = pl.ds(pl.multiple_of(k * depth, depth), depth)
        raw_cot[...] += contract_cols(slot_cot[:, cols], w_down[:, cols])

    gather_and_dispatch(here, sender, over_e, hidden_ref, select_t, rows, rows_of)

    @pl.loop(0, slots // 16)
    def _(k):
        block = pl.ds(pl.multiple_of(k * 16, 16), 16)
        value = rows[block, :].astype(F32)
        inv_rms = lax.rsqrt(jnp.mean(value * value, axis=1, keepdims=True) + 1e-05)
        normed = (value * inv_rms * gain_ref[...]).astype(BF16)
        own_in[block, :] = normed
        logit = jnp.sum(normed.astype(F32) * router_ref[...], axis=1, keepdims=True)
        gate = jax.nn.sigmoid(logit)
        gates[block, :] = gate
        out_cot_ref[block, :] = (gate * slot_cot[block, :].astype(F32)).astype(BF16)

    loads[1].wait()
    loads[2].wait()
    pre_gate[...] = jnp.zeros_like(pre_gate)
    pre_up[...] = jnp.zeros_like(pre_up)

    @pl.loop(0, steps)
    def _(k):
        cols = pl.ds(pl.multiple_of(k * depth, depth), depth)
        pre_gate[...] += jnp.dot(own_in[:, cols], w_gate[cols, :], preferred_element_type=F32)
        pre_up[...] += jnp.dot(own_in[:, cols], w_up[cols, :], preferred_element_type=F32)

    @pl.loop(0, slots // 16)
    def _(k):
        block = pl.ds(pl.multiple_of(k * 16, 16), 16)
        gate, raw = gates[block, :], raw_cot[block, :]
        z, up = pre_gate[block, :], pre_up[block, :]
        sig = jax.nn.sigmoid(z)
        act = (z * sig * up).astype(BF16)
        act_ref[block, :] = act
        act_cot = gate * raw
        d_gate[block, :] = (act_cot * up * sig * (1.0 + z * (1.0 - sig))).astype(BF16)
        d_up[block, :] = (act_cot * z * sig).astype(BF16)
        gate_cot = jnp.sum(act.astype(F32) * raw, axis=1, keepdims=True)
        slopes[block, :] = gate_cot * gate * (1.0 - gate)

    span, spans = tiles(here.quarter, 512)

    def forward_tile(cols):
        own_out[:, cols] = (
            gates[...] * jnp.dot(act_ref[...], w_down[:, cols], preferred_element_type=F32)
        ).astype(BF16)

    def backward_tile(cols):
        own_in[:, cols] = (
            contract_cols(d_gate[...], w_gate[cols, :])
            + contract_cols(d_up[...], w_up[cols, :])
            + slopes[...] * router_ref[:, cols]
        ).astype(BF16)

    crossing = {}
    for i, (source, tile) in enumerate(((own_out, forward_tile), (own_in, backward_tile))):

        def fill(h, c, tile=tile):
            first = c * here.half + h * here.quarter

            @pl.loop(0, spans)
            def _(k):
                tile(pl.ds(pl.multiple_of(first + k * span, span), span))

        swaps = {}
        for flip in (1, 0):
            h = lax.rem(here.h + flip, 2)
            fill(h, 1 - here.c)
            for k, (d, f) in enumerate(plane):
                if f == flip:
                    swaps[k] = sender.start(
                        source.at[rows_of(here.step_x(d)), here.cols_h(h, 1 - here.c)],
                        pair_in.at[i, k],
                        here.device(c=1 - here.c),
                    )
        for flip in (1, 0):
            h = lax.rem(here.h + flip, 2)
            fill(h, here.c)
            for k, (d, f) in enumerate(plane):
                if f == flip:
                    swaps[k].wait_recv()
                    paired[i, k] = (
                        source[rows_of(here.step_x(d)), here.cols_h(h, here.c)].astype(F32)
                        + pair_in[i, k].astype(F32)
                    ).astype(BF16)
                    if d or f:
                        crossing[i, k] = sender.start(
                            paired.at[i, k], parts.at[i, k], here.device(x=here.step_x(d), h=h)
                        )

    own_slot = plane.index((0, 0))
    scattered = {}
    for i in range(2):
        total = paired[i, own_slot].astype(F32)
        for k in range(len(plane)):
            if k != own_slot:
                crossing[i, k].wait_recv()
                total = total + parts[i, k].astype(F32)
        tokens[i] = jnp.dot(
            select_ref[...], total.astype(BF16), preferred_element_type=F32
        ).astype(BF16)
        for d in range(1, experts):
            e = here.step_e(d)
            cols = pl.ds(pl.multiple_of(e * here.piece, here.piece), here.piece)
            scattered[i, d] = sender.start(
                tokens.at[i, :, cols], pieces.at[i, d - 1], here.device(e=e)
            )
    mine_cols = pl.ds(pl.multiple_of(here.e * here.piece, here.piece), here.piece)
    started = []
    for i, result in enumerate((mix_ref, cot_ref)):
        total = tokens[i, :, mine_cols].astype(F32)
        for d in range(1, experts):
            scattered[i, d].wait_recv()
            total = total + pieces[i, d - 1].astype(F32)
        result[:, own_cols] = total.astype(BF16)
        started.append((result, gather_start(here, sender, result)))
    gather_rest(here, sender, started)
    sender.finish()


def on_device(
    n_dp, resid, mixer_out, out_proj, norm_gain, router, routes, w_gate, w_up, w_down, cotangent
):
    row_count, width = resid.shape
    experts = router.shape[1]
    capacity = min(row_count, 3 * row_count // experts)
    half, quarter, piece = width // 2, width // 4, width // (4 * experts)
    expert_id = lax.axis_index("tensor") // 2

    hit = jnp.any(routes == expert_id, axis=1)
    earlier = jnp.arange(row_count)[None, :] < jnp.arange(row_count)[:, None]
    slot_pos = jnp.sum((earlier & hit[None, :]).astype(jnp.int32), axis=1)
    select = (
        hit[:, None] & (slot_pos[:, None] == jnp.arange(capacity, dtype=jnp.int32)[None, :])
    ).astype(BF16)
    local_cots = contract_rows(select, cotangent).astype(BF16)

    own_term = jnp.dot(mixer_out, out_proj, preferred_element_type=F32).astype(BF16)
    slots, units, plane = n_dp * capacity, w_gate.shape[2], 2 * n_dp
    router_row = lax.dynamic_slice_in_dim(router, expert_id, 1, 1).T
    gathers = 4 * experts - 1
    dispatch = 4 * experts * (n_dp - 1)
    reduce = 1 + 2 * (n_dp - 1) + 2 * experts - 1
    combine = 2 * (plane + plane - 1 + experts - 1 + gathers)
    copies = reduce + gathers + dispatch + combine
    whole = pl.BlockSpec(memory_space=pltpu.VMEM)
    remote = pl.BlockSpec(memory_space=pl.ANY)
    hidden_bf, mixture, normed_cot, activated, out_cot = pl.pallas_call(
        functools.partial(layer_kernel, n_dp, experts),
        out_shape=[jax.ShapeDtypeStruct((row_count, width), BF16)] * 3
        + [
            jax.ShapeDtypeStruct((slots, units), BF16),
            jax.ShapeDtypeStruct((slots, width), BF16),
        ],
        in_specs=[whole] * 7 + [remote] * 3,
        out_specs=[whole] * 5,
        scratch_shapes=[
            pltpu.VMEM((width, units), BF16),
            pltpu.VMEM((width, units), BF16),
            pltpu.VMEM((units, width), BF16),
            pltpu.VMEM((slots, width), BF16),
            pltpu.VMEM((slots, width), BF16),
            pltpu.VMEM((slots, width), BF16),
            pltpu.VMEM((slots, width), BF16),
            pltpu.VMEM((row_count, half), BF16),
            pltpu.VMEM((row_count, half), BF16),
            pltpu.VMEM((2 * experts - 1, row_count, piece), BF16),
            pltpu.VMEM((2, plane, capacity, quarter), BF16),
            pltpu.VMEM((2, plane, capacity, quarter), BF16),
            pltpu.VMEM((2, plane, capacity, quarter), BF16),
            pltpu.VMEM((2, row_count, quarter), BF16),
            pltpu.VMEM((2, experts - 1, row_count, piece), BF16),
            pltpu.VMEM((slots, units), BF16),
            pltpu.VMEM((slots, units), BF16),
            pltpu.VMEM((slots, units), F32),
            pltpu.VMEM((slots, units), F32),
            pltpu.VMEM((slots, units), F32),
            pltpu.VMEM((slots, 1), F32),
            pltpu.VMEM((slots, 1), F32),
            pltpu.SemaphoreType.DMA((3,)),
            pltpu.SemaphoreType.DMA((copies,)),
            pltpu.SemaphoreType.DMA((copies,)),
        ],
        compiler_params=pltpu.CompilerParams(
            collective_id=0, has_side_effects=True, vmem_limit_bytes=VMEM_MIB * 1024 * 1024
        ),
    )(
        own_term,
        local_cots,
        select,
        select.T,
        resid,
        norm_gain[None],
        router_row,
        w_gate[0],
        w_up[0],
        w_down[0],
    )
    grad_down = contract_rows(activated, out_cot).astype(BF16)[None]
    hidden = hidden_bf.astype(F32)
    inv_rms = lax.rsqrt(jnp.mean(hidden * hidden, axis=1, keepdims=True) + 1e-05)
    layer_out = (hidden + mixture.astype(F32)).astype(BF16)
    hidden_cot = (
        cotangent.astype(F32)
        + norm_backward(hidden, inv_rms, norm_gain, normed_cot.astype(F32))
    ).astype(BF16)
    grad_mixer = contract_cols(hidden_cot, out_proj).astype(BF16)
    return (layer_out, grad_mixer, grad_down)


def solution(mesh):
    placed = (
        P("dp", None),
        P("dp", ("tensor", "group")),
        P(("tensor", "group"), None),
        P(),
        P(),
        P("dp", None),
        P("tensor", None, ("dp", "group")),
        P("tensor", None, ("dp", "group")),
        P("tensor", ("dp", "group"), None),
        P("dp", None),
    )
    return jax.shard_map(
        functools.partial(on_device, mesh.shape["dp"]),
        mesh=mesh,
        in_specs=placed,
        out_specs=(P("dp", None), P("dp", ("tensor", "group")), P("tensor", ("dp", "group"), None)),
        check_vma=False,
    )
```

time: 431 us -> 122 us (0.28)
  waiting for transfers between devices: 292 us -> 0 us
  Pallas kernels: 0 us -> 97.9 us
  matrix products: 61.2 us -> 15.5 us
  local copies, waits for them, and re-layouts: 30.2 us -> 1.49 us
  other arithmetic: 31.6 us -> 5.9 us
  between operations: 14.4 us -> 0.72 us
    all_gather x4 -> x0, waiting for transfers between devices: 142 us -> none  [the longest x2 89.5 us: join_experts(): gathered = lax.all_gather(half_out, ('tensor', 'group'), axis=0, tiled=True)]
    pallas_call x0 -> x1, Pallas kernels: none -> 97.9 us  [on_device(): pl.pallas_call(functools.partial(layer_kernel, n_dp, experts), out_shape=...]
    psum x1 -> x0, waiting for transfers between devices: 93.9 us -> none  [on_device(): lax.psum(own_term.astype(jnp.bfloat16), ('tensor', 'group'))]
    reduce_scatter x2 -> x0, waiting for transfers between devices: 56.6 us -> none  [the longest x1 28.3 us: on_device(): lax.psum_scatter(jnp.dot(activated, w_down[0], preferred_element_type=jnp...]
    dot_general x7 -> x1, matrix products: 29.6 us -> 3.88 us  [on_device(): jnp.dot(mixer_out, out_proj, preferred_element_type=F32).astype(BF16)]
    reshape x4 -> x0, local copies, waits for them, and re-layouts: 16.2 us -> none  [the longest x1 6.14 us: on_device(): pair_cot = jnp.repeat(cot_full, 2, axis=0)]
    dot_general x4 -> x1, matrix products: 18.2 us -> 3.89 us  [contract_cols(): lax.dot_general(left, right, (((1,), (1,)), ((), ())), preferred_element_...]
    convert_element_type x7 -> x2, other arithmetic: 14.2 us -> 1.33 us  [on_device(): select = (hit[:, None] & (slot_pos[:, None] == jnp.arange(capacity, dtype...]
  transfers between devices with their start and end apart: 7 -> 0, of which waited for: 7 -> 0; matrix products, arithmetic and copies ran while one was open for 9% -> 0% of each run, Pallas kernels for 0% -> 0%
where the time goes in v1:
time: 122 us
  Pallas kernels  97.9 us (80%)
  matrix products  15.5 us (13%)
  other arithmetic  5.9 us (5%)
  local copies, waits for them, and re-layouts  1.49 us (1%)
    pallas_call x1, Pallas kernels, on_device(): pl.pallas_call(functools.partial(layer_kernel, n_dp, experts), out_shape=...  97.9 us
    dot_general x2, matrix products, contract_rows(): lax.dot_general(left, right, (((0,), (0,)), ((), ())), preferred_element_...  7.77 us
    dot_general x1, matrix products, contract_cols(): lax.dot_general(left, right, (((1,), (1,)), ((), ())), preferred_element_...  3.89 us
    dot_general x1, matrix products, on_device(): jnp.dot(mixer_out, out_proj, preferred_element_type=F32).astype(BF16)  3.88 us
    reduce_sum x1, other arithmetic, on_device(): jnp.mean(hidden * hidden, axis=1, keepdims=True) + 1e-05  3.71 us

profile of v1, /device:TPU:0, one launch (start us, length us, event | category | flops | bytes accessed | tf_op | source)
XLA Modules:
  0.0 121.6 jit_solution(8871399161647001576)
XLA Ops:
  0.6 0.0 copy-start
  0.7 0.7 compare_reduce_fusion
  1.4 0.1 convert_reduce_fusion
  1.5 1.5 %dynamic-slice_bitcast_fusion.router_ref = f32[1,4096]{1,0:T(1,128)} fusion(f32[4096,4]{0,1:T(4,128)} %param.14, s32[]{:T(128)S(6)} %select_n.9), kind=kLoop, calls=%fused_computation.31 | loop fusion | bytes 32772 | tf_op jit(solution)/shard_map/transpose | solution.py:429
  3.0 0.6 fusion.17.select_t
  3.6 0.7 fusion.14.select_ref
  4.3 2.6 %convolution_convert_fusion.1.cots_ref = bf16[96,4096]{1,0:T(8,128)(2,1)} fusion(bf16[128,4096]{1,0:T(8,128)(2,1)} %param.19, s32[128]{0:T(128)S(1)} %convert_reduce_fusion, pred[128]{0:T(512)(128)(4,1)S(1)} %compare_reduce_fusion), kind=kOutput, calls=%fused_computation.2 | convolution fusion | flops 101081088 | bytes 1835648 | tf_op jit(solution)/shard_map/dot_general | solution.py:17
  6.9 0.0 copy-done
  6.9 3.9 %convolution_convert_fusion.own_ref = bf16[128,4096]{1,0:T(8,128)(2,1)} fusion(bf16[128,512]{1,0:T(8,128)(2,1)S(1)} %copy-done, bf16[512,4096]{1,0:T(8,128)(2,1)} %param.12), kind=kOutput, calls=%fused_computation.1 | convolution fusion | flops 537395200 | bytes 5373952 | tf_op jit(solution)/shard_map/dot_general | solution.py:427
  10.8 0.0 copy-start.5
  10.8 0.0 copy-start.3
  10.8 97.9 %shard_map.121 = (bf16[128,4096]{1,0:T(8,128)(2,1)}, bf16[128,4096]{1,0:T(8,128)(2,1)}, bf16[128,4096]{1,0:T(8,128)(2,1)}, bf16[192,896]{1,0:T(8,128)(2,1)}, bf16[192,4096]{1,0:T(8,128)(2,1)}) custom-call(bf16[128,4096]{1,0:T(8,128)(2,1)} %convolution_convert_fusion.own_ref, bf16[96,4096]{1,0:T(8,128)(2,1)} %convolution_convert_fusion.1.cots_ref, ...), custom_call_target="tpu_custom_call" | custom-call | tf_op jit(solution)/shard_map/pallas_call | solution.py:437
  108.7 0.0 copy-done.5
  108.7 0.0 copy-start.1
  108.8 3.7 %fusion.1 = (f32[128]{0:T(128)S(1)}, f32[128]{0:T(128)S(1)}, bf16[128,4096]{1,0:T(8,128)(2,1)}) fusion(bf16[128,4096]{1,0:T(8,128)(2,1)} %get-tuple-element.8, f32[4096]{0:T(1024)S(1)} %copy-done.5, bf16[128,4096]{1,0:T(8,128)(2,1)} %get-tuple-element.10, bf16[128,4096]{1,0:T(8,128)(2,1)} %get-tuple-element.9), kind=kLoop, calls=%fused_computation.8 | loop fusion | flops 5242624 | bytes 4211712 | tf_op jit(solution)/shard_map/reduce_sum | solution.py:490
  112.5 0.0 copy-done.3
  112.5 0.0 copy-done.1
  112.5 0.0 copy-start.2
  112.5 0.0 copy-start.4
  112.5 3.9 %convolution_convert_fusion.2 = bf16[128,512]{1,0:T(8,128)(2,1)} fusion(bf16[512,4096]{1,0:T(8,128)(2,1)S(1)} %copy-done.1, bf16[128,4096]{1,0:T(8,128)(2,1)} %get-tuple-element.8, bf16[128,4096]{1,0:T(8,128)(2,1)} %get-tuple-element.10, bf16[128,4096]{1,0:T(8,128)(2,1)S(1)} %copy-done.3, f32[128]{0:T(128)S(1)} %get-tuple-element.18, ...), kind=kOutput, calls=%fused_computation.15 | convolution fusion | flops 542179328 | bytes 7489024 | tf_op jit(solution)/shard_map/dot_general | solution.py:21
  116.4 0.0 copy-done.2
  116.4 0.0 copy-done.4
  116.4 5.2 %convert_bitcast_fusion = bf16[1,896,4096]{2,1,0:T(8,128)(2,1)} fusion(bf16[192,896]{1,0:T(8,128)(2,1)S(1)} %copy-done.4, bf16[192,4096]{1,0:T(8,128)(2,1)S(1)} %copy-done.2), kind=kOutput, calls=%fused_computation | convolution fusion | flops 1412956160 | bytes 9256960 | tf_op jit(solution)/shard_map/dot_general | solution.py:17
  (1 shorter events, 0.0 us)
Async XLA Ops:
  0.6 6.3 %copy-start = (bf16[128,512]{1,0:T(8,128)(2,1)S(1)}, bf16[128,512]{1,0:T(8,128)(2,1)}, u32[]{:S(2)}) copy-start(bf16[128,512]{1,0:T(8,128)(2,1)} %param.11) | copy-start | bytes 393220
  10.8 98.0 %copy-start.5 = (f32[4096]{0:T(1024)S(1)}, f32[4096]{0:T(1024)}, u32[]{:S(2)}) copy-start(f32[4096]{0:T(1024)} %param.13) | copy-start | bytes 49156
  10.8 101.7 %copy-start.3 = (bf16[128,4096]{1,0:T(8,128)(2,1)S(1)}, bf16[128,4096]{1,0:T(8,128)(2,1)}, u32[]{:S(2)}) copy-start(bf16[128,4096]{1,0:T(8,128)(2,1)} %param.19) | copy-start | bytes 3145732
  108.7 3.7 %copy-start.1 = (bf16[512,4096]{1,0:T(8,128)(2,1)S(1)}, bf16[512,4096]{1,0:T(8,128)(2,1)}, u32[]{:S(2)}) copy-start(bf16[512,4096]{1,0:T(8,128)(2,1)} %param.12) | copy-start | bytes 12582916
  112.5 3.9 %copy-start.2 = (bf16[192,4096]{1,0:T(8,128)(2,1)S(1)}, bf16[192,4096]{1,0:T(8,128)(2,1)}, u32[]{:S(2)}) copy-start(bf16[192,4096]{1,0:T(8,128)(2,1)} %get-tuple-element.12) | copy-start | bytes 4718596
  112.5 3.9 %copy-start.4 = (bf16[192,896]{1,0:T(8,128)(2,1)S(1)}, bf16[192,896]{1,0:T(8,128)(2,1)}, u32[]{:S(2)}) copy-start(bf16[192,896]{1,0:T(8,128)(2,1)} %get-tuple-element.11) | copy-start | bytes 1032196

commit v2 on v1

--- a/solution.py
+++ b/solution.py
@@ -10,7 +10,7 @@
 MESH = pl.DeviceIdType.MESH
 F32 = jnp.float32
 BF16 = jnp.bfloat16
-VMEM_MIB = 56
+VMEM_MIB = 60
 
 
 def contract_rows(left, right):
@@ -19,12 +19,6 @@
 
 def contract_cols(left, right):
     return lax.dot_general(left, right, (((1,), (1,)), ((), ())), preferred_element_type=F32)
-
-
-def norm_backward(hidden, inv_rms, norm_gain, normed_cot):
-    weighted = normed_cot * norm_gain
-    inner_mean = jnp.mean(weighted * hidden, axis=1, keepdims=True)
-    return inv_rms * weighted - inv_rms * inv_rms * inv_rms * hidden * inner_mean
 
 
 class Place:
@@ -101,21 +95,24 @@
     ]
 
 
-def gather_rest(place, sender, started):
+def gather_pass(place, sender, out, over_e):
     here = place
-    over_h, over_c = {}, []
+    over_h, over_c = [], []
     for d in range(here.experts):
         where = (slice(None), here.cols_e(here.step_e(-d), here.h, here.c))
-        for i, (out, over_e) in enumerate(started):
-            if d:
-                over_e[d].wait_recv()
-            over_h[i, d] = forward(here, sender, out, where, h=1 - here.h)
-            over_c.append(forward(here, sender, out, where, c=1 - here.c))
+        if d:
+            over_e[d].wait_recv()
+        over_h.append(forward(here, sender, out, where, h=1 - here.h))
+        over_c.append(forward(here, sender, out, where, c=1 - here.c))
+    return over_h, over_c
+
+
+def gather_finish(place, sender, out, over_h, over_c):
+    here = place
     for d in range(here.experts):
         where = (slice(None), here.cols_e(here.step_e(-d), 1 - here.h, here.c))
-        for i, (out, over_e) in enumerate(started):
-            over_h[i, d].wait_recv()
-            over_c.append(forward(here, sender, out, where, c=1 - here.c))
+        over_h[d].wait_recv()
+        over_c.append(forward(here, sender, out, where, c=1 - here.c))
     for copy in over_c:
         copy.wait_recv()
 
@@ -161,8 +158,7 @@
     for copy in over_c:
         copy.wait_recv()
     pick(here.cols_c(1 - here.c))
-    for copy in rows_c:
-        copy.wait_recv()
+    return rows_c
 
 
 def tiles(extent, most):
@@ -175,30 +171,39 @@
 def layer_kernel(
     n_dp,
     experts,
-    own_ref,
-    cots_ref,
-    select_ref,
-    select_t,
+    mixer_ref,
+    routes_ref,
+    routes_t,
+    cotangent_ref,
     resid_ref,
     gain_ref,
     router_ref,
     gate_hbm,
     up_hbm,
     down_hbm,
-    hidden_ref,
-    mix_ref,
-    cot_ref,
+    proj_hbm,
+    layer_ref,
+    mixer_cot_ref,
     act_ref,
     out_cot_ref,
     w_gate,
     w_up,
     w_down,
+    w_proj,
+    own,
+    hidden,
+    mix,
+    cot,
+    select,
+    select_t,
     slot_cot,
     rows,
     own_out,
     own_in,
     swap_in,
     swapped,
+    half_in,
+    half_sum,
     hidden_parts,
     pair_in,
     paired,
@@ -212,17 +217,16 @@
     pre_up,
     gates,
     slopes,
+    hidden_cot,
     load_sems,
     send_sems,
     recv_sems,
 ):
-    width = own_ref.shape[1]
-    capacity = cots_ref.shape[0]
-    slots = n_dp * capacity
+    row_count, width = resid_ref.shape
+    slots = slot_cot.shape[0]
+    capacity = slots // n_dp
     here = Place(n_dp, experts, width)
     sender = Sender(send_sems, recv_sems)
-    tensor = 2 * experts
-    mine = 2 * here.e + here.h
 
     def rows_of(x):
         return pl.ds(pl.multiple_of(x * capacity, capacity), capacity)
@@ -231,51 +235,101 @@
         pltpu.make_async_copy(src, dst, load_sems.at[k])
         for k, (src, dst) in enumerate(((down_hbm, w_down), (gate_hbm, w_gate), (up_hbm, w_up)))
     ]
+    blocks = [(flip, other) for other in (1, 0) for flip in (1, 0)]
+    proj_loads = []
+    for k, (flip, other) in enumerate(blocks):
+        cols = here.cols_h(lax.rem(here.h + flip, 2), lax.rem(here.c + other, 2))
+        load = pltpu.make_async_copy(
+            proj_hbm.at[:, cols], w_proj.at[:, cols], load_sems.at[3 + k]
+        )
+        load.start()
+        proj_loads.append((cols, load))
+
+    plane = [(d, flip) for flip in (1, 0) for d in range(n_dp)]
+    devices = [here.device(c=1 - here.c)]
+    devices += [here.device(e=here.step_e(d)) for d in range(1, experts)]
+    devices += [
+        here.device(x=here.step_x(d), h=lax.rem(here.h + flip, 2)) for d, flip in plane if d or flip
+    ]
+    greet(devices)
+
+    hit = ((routes_ref[:, 0:1] == here.e) | (routes_ref[:, 1:2] == here.e)).astype(F32)
+    hit_t = ((routes_t[0:1, :] == here.e) | (routes_t[1:2, :] == here.e)).astype(F32)
+    row = lax.broadcasted_iota(jnp.int32, (row_count, row_count), 0)
+    col = lax.broadcasted_iota(jnp.int32, (row_count, row_count), 1)
+    slot = jnp.sum(jnp.where(col < row, hit_t, 0.0), axis=1, keepdims=True)
+    slot_t = jnp.sum(jnp.where(row < col, hit, 0.0), axis=0, keepdims=True)
+    number = lax.broadcasted_iota(jnp.int32, (row_count, capacity), 1).astype(F32)
+    number_t = lax.broadcasted_iota(jnp.int32, (capacity, row_count), 0).astype(F32)
+    select[...] = jnp.where(slot == number, hit, 0.0).astype(BF16)
+    select_t[...] = jnp.where(slot_t == number_t, hit_t, 0.0).astype(BF16)
+
+    half_cols = here.cols_c(here.c)
+    own_rows = rows_of(here.x)
+
+    def pick_cot(cols):
+        slot_cot[own_rows, cols] = jnp.dot(
+            select_t[...], cotangent_ref[:, cols], preferred_element_type=F32
+        ).astype(BF16)
+
+    pick_cot(half_cols)
+    replicas = [
+        forward(here, sender, slot_cot, (own_rows, half_cols), x=here.step_x(d))
+        for d in range(1, n_dp)
+    ]
+
+    swaps = []
+    for (flip, other), (cols, load) in zip(blocks, proj_loads):
+        load.wait()
+        own[:, cols] = jnp.dot(
+            mixer_ref[...], w_proj[:, cols], preferred_element_type=F32
+        ).astype(BF16)
+        if other:
+            there = here.cols_h(lax.rem(here.h + flip, 2), 0)
+            swaps.append(
+                sender.start(own.at[:, cols], swap_in.at[:, there], here.device(c=1 - here.c))
+            )
     for load in loads:
         load.start()
-
-    peers = []
-    for d in range(1, tensor):
-        other = lax.rem(mine + d, tensor)
-        peers.append((other // 2, lax.rem(other, 2)))
-    plane = [(d, flip) for flip in (1, 0) for d in range(n_dp)]
-    devices = [here.device(c=1 - here.c)]
-    devices += [here.device(e=e, h=h) for e, h in peers]
-    devices += [
-        here.device(x=here.step_x(d), h=lax.rem(here.h + flip, 2)) for d, flip in plane if d
-    ]
-    greet(devices)
-
-    swap = sender.start(own_ref.at[:, here.cols_c(1 - here.c)], swap_in, here.device(c=1 - here.c))
-    half_cols = here.cols_c(here.c)
-    replicas = [
-        sender.start(
-            cots_ref.at[:, half_cols],
-            slot_cot.at[rows_of(here.x), half_cols],
-            here.device(x=here.step_x(d)),
-        )
-        for d in range(1, n_dp)
-    ]
-    swap.wait_recv()
-    swapped[...] = (own_ref[:, half_cols].astype(F32) + swap_in[...].astype(F32)).astype(BF16)
-    arrivals = [
-        sender.start(swapped.at[:, here.cols_e(e, h, 0)], hidden_parts.at[d], here.device(e=e, h=h))
-        for d, (e, h) in enumerate(peers)
-    ]
-    slot_cot[rows_of(here.x), :] = cots_ref[...]
+    order = list(range(1, experts)) + [0]
+    halves = {}
+    for flip in (1, 0):
+        h = lax.rem(here.h + flip, 2)
+        there = here.cols_h(h, 0)
+        swaps[1 - flip].wait_recv()
+        swapped[:, there] = (
+            own[:, here.cols_h(h, here.c)].astype(F32) + swap_in[:, there].astype(F32)
+        ).astype(BF16)
+        if flip:
+            for d in order:
+                halves[d] = sender.start(
+                    swapped.at[:, here.cols_e(here.step_e(d), h, 0)],
+                    half_in.at[d],
+                    here.device(h=h),
+                )
+    pick_cot(here.cols_c(1 - here.c))
+    arrivals = {}
+    for d in order:
+        halves[d].wait_recv()
+        total = swapped[:, here.cols_e(here.step_e(d), here.h, 0)].astype(F32)
+        total = total + half_in[d].astype(F32)
+        if d:
+            half_sum[d - 1] = total.astype(BF16)
+            arrivals[d] = sender.start(
+                half_sum.at[d - 1], hidden_parts.at[d - 1], here.device(e=here.step_e(d))
+            )
     shared = []
     for d in range(1, n_dp):
         replicas[d - 1].wait_recv()
         where = (rows_of(here.step_x(-d)), half_cols)
         shared.append(forward(here, sender, slot_cot, where, c=1 - here.c))
     own_cols = here.cols_e(here.e, here.h, here.c)
-    total = swapped[:, here.cols_e(here.e, here.h, 0)].astype(F32)
     total = total + resid_ref[:, own_cols].astype(F32)
-    for d, copy in enumerate(arrivals):
-        copy.wait_recv()
-        total = total + hidden_parts[d].astype(F32)
-    hidden_ref[:, own_cols] = total.astype(BF16)
-    over_e = gather_start(here, sender, hidden_ref)
+    for d in range(1, experts):
+        arrivals[d].wait_recv()
+        total = total + hidden_parts[d - 1].astype(F32)
+    hidden[:, own_cols] = total.astype(BF16)
+    over_e = gather_start(here, sender, hidden)
 
     for copy in shared:
         copy.wait_recv()
@@ -288,19 +342,27 @@
         cols = pl.ds(pl.multiple_of(k * depth, depth), depth)
         raw_cot[...] += contract_cols(slot_cot[:, cols], w_down[:, cols])
 
-    gather_and_dispatch(here, sender, over_e, hidden_ref, select_t, rows, rows_of)
-
-    @pl.loop(0, slots // 16)
-    def _(k):
-        block = pl.ds(pl.multiple_of(k * 16, 16), 16)
-        value = rows[block, :].astype(F32)
-        inv_rms = lax.rsqrt(jnp.mean(value * value, axis=1, keepdims=True) + 1e-05)
-        normed = (value * inv_rms * gain_ref[...]).astype(BF16)
-        own_in[block, :] = normed
-        logit = jnp.sum(normed.astype(F32) * router_ref[...], axis=1, keepdims=True)
-        gate = jax.nn.sigmoid(logit)
-        gates[block, :] = gate
-        out_cot_ref[block, :] = (gate * slot_cot[block, :].astype(F32)).astype(BF16)
+    router_row = router_ref.at[pl.ds(here.e, 1), :]
+    rows_c = gather_and_dispatch(here, sender, over_e, hidden, select_t, rows, rows_of)
+
+    def norm_rows(x):
+        @pl.loop(0, capacity // 16)
+        def _(k):
+            block = pl.ds(pl.multiple_of(x * capacity + k * 16, 16), 16)
+            value = rows[block, :].astype(F32)
+            inv_rms = lax.rsqrt(jnp.mean(value * value, axis=1, keepdims=True) + 1e-05)
+            normed = (value * inv_rms * gain_ref[...]).astype(BF16)
+            own_in[block, :] = normed
+            logit = jnp.sum(normed.astype(F32) * router_row[...], axis=1, keepdims=True)
+            gate = jax.nn.sigmoid(logit)
+            gates[block, :] = gate
+            out_cot_ref[block, :] = (gate * slot_cot[block, :].astype(F32)).astype(BF16)
+
+    norm_rows(here.x)
+    for copy in rows_c:
+        copy.wait_recv()
+    for d in range(1, n_dp):
+        norm_rows(here.step_x(d))
 
     loads[1].wait()
     loads[2].wait()
@@ -338,7 +400,7 @@
         own_in[:, cols] = (
             contract_cols(d_gate[...], w_gate[cols, :])
             + contract_cols(d_up[...], w_up[cols, :])
-            + slopes[...] * router_ref[:, cols]
+            + slopes[...] * router_row[:, cols]
         ).astype(BF16)
 
     crossing = {}
@@ -378,32 +440,55 @@
                         )
 
     own_slot = plane.index((0, 0))
-    scattered = {}
-    for i in range(2):
+    mine_cols = pl.ds(pl.multiple_of(here.e * here.piece, here.piece), here.piece)
+    started = []
+    for i, result in enumerate((mix, cot)):
         total = paired[i, own_slot].astype(F32)
         for k in range(len(plane)):
             if k != own_slot:
                 crossing[i, k].wait_recv()
                 total = total + parts[i, k].astype(F32)
-        tokens[i] = jnp.dot(
-            select_ref[...], total.astype(BF16), preferred_element_type=F32
-        ).astype(BF16)
+        tokens[i] = jnp.dot(select[...], total.astype(BF16), preferred_element_type=F32).astype(
+            BF16
+        )
+        scattered = []
         for d in range(1, experts):
             e = here.step_e(d)
             cols = pl.ds(pl.multiple_of(e * here.piece, here.piece), here.piece)
-            scattered[i, d] = sender.start(
-                tokens.at[i, :, cols], pieces.at[i, d - 1], here.device(e=e)
+            scattered.append(
+                sender.start(tokens.at[i, :, cols], pieces.at[i, d - 1], here.device(e=e))
             )
-    mine_cols = pl.ds(pl.multiple_of(here.e * here.piece, here.piece), here.piece)
-    started = []
-    for i, result in enumerate((mix_ref, cot_ref)):
+        if i:
+            mix_passed = gather_pass(here, sender, mix, started[0])
         total = tokens[i, :, mine_cols].astype(F32)
         for d in range(1, experts):
-            scattered[i, d].wait_recv()
+            scattered[d - 1].wait_recv()
             total = total + pieces[i, d - 1].astype(F32)
         result[:, own_cols] = total.astype(BF16)
-        started.append((result, gather_start(here, sender, result)))
-    gather_rest(here, sender, started)
+        started.append(gather_start(here, sender, result))
+    cot_passed = gather_pass(here, sender, cot, started[1])
+    gather_finish(here, sender, mix, *mix_passed)
+
+    @pl.loop(0, row_count // 16)
+    def _(k):
+        block = pl.ds(pl.multiple_of(k * 16, 16), 16)
+        layer_ref[block, :] = (hidden[block, :].astype(F32) + mix[block, :].astype(F32)).astype(
+            BF16
+        )
+
+    gather_finish(here, sender, cot, *cot_passed)
+
+    @pl.loop(0, row_count // 16)
+    def _(k):
+        block = pl.ds(pl.multiple_of(k * 16, 16), 16)
+        value = hidden[block, :].astype(F32)
+        inv_rms = lax.rsqrt(jnp.mean(value * value, axis=1, keepdims=True) + 1e-05)
+        weighted = cot[block, :].astype(F32) * gain_ref[...]
+        inner_mean = jnp.mean(weighted * value, axis=1, keepdims=True)
+        change = inv_rms * weighted - inv_rms * inv_rms * inv_rms * value * inner_mean
+        hidden_cot[block, :] = (cotangent_ref[block, :].astype(F32) + change).astype(BF16)
+
+    mixer_cot_ref[...] = contract_cols(hidden_cot[...], w_proj[...]).astype(BF16)
     sender.finish()
 
 
@@ -414,46 +499,44 @@
     experts = router.shape[1]
     capacity = min(row_count, 3 * row_count // experts)
     half, quarter, piece = width // 2, width // 4, width // (4 * experts)
-    expert_id = lax.axis_index("tensor") // 2
-
-    hit = jnp.any(routes == expert_id, axis=1)
-    earlier = jnp.arange(row_count)[None, :] < jnp.arange(row_count)[:, None]
-    slot_pos = jnp.sum((earlier & hit[None, :]).astype(jnp.int32), axis=1)
-    select = (
-        hit[:, None] & (slot_pos[:, None] == jnp.arange(capacity, dtype=jnp.int32)[None, :])
-    ).astype(BF16)
-    local_cots = contract_rows(select, cotangent).astype(BF16)
-
-    own_term = jnp.dot(mixer_out, out_proj, preferred_element_type=F32).astype(BF16)
     slots, units, plane = n_dp * capacity, w_gate.shape[2], 2 * n_dp
-    router_row = lax.dynamic_slice_in_dim(router, expert_id, 1, 1).T
     gathers = 4 * experts - 1
     dispatch = 4 * experts * (n_dp - 1)
-    reduce = 1 + 2 * (n_dp - 1) + 2 * experts - 1
+    reduce = 2 + 2 * (n_dp - 1) + 2 * experts - 1
     combine = 2 * (plane + plane - 1 + experts - 1 + gathers)
     copies = reduce + gathers + dispatch + combine
     whole = pl.BlockSpec(memory_space=pltpu.VMEM)
     remote = pl.BlockSpec(memory_space=pl.ANY)
-    hidden_bf, mixture, normed_cot, activated, out_cot = pl.pallas_call(
+    layer_out, grad_mixer, activated, out_cot = pl.pallas_call(
         functools.partial(layer_kernel, n_dp, experts),
-        out_shape=[jax.ShapeDtypeStruct((row_count, width), BF16)] * 3
-        + [
+        out_shape=[
+            jax.ShapeDtypeStruct((row_count, width), BF16),
+            jax.ShapeDtypeStruct(mixer_out.shape, BF16),
             jax.ShapeDtypeStruct((slots, units), BF16),
             jax.ShapeDtypeStruct((slots, width), BF16),
         ],
-        in_specs=[whole] * 7 + [remote] * 3,
-        out_specs=[whole] * 5,
+        in_specs=[whole] * 7 + [remote] * 4,
+        out_specs=[whole] * 4,
         scratch_shapes=[
             pltpu.VMEM((width, units), BF16),
             pltpu.VMEM((width, units), BF16),
             pltpu.VMEM((units, width), BF16),
+            pltpu.VMEM(out_proj.shape, BF16),
+            pltpu.VMEM((row_count, width), BF16),
+            pltpu.VMEM((row_count, width), BF16),
+            pltpu.VMEM((row_count, width), BF16),
+            pltpu.VMEM((row_count, width), BF16),
+            pltpu.VMEM((row_count, capacity), BF16),
+            pltpu.VMEM((capacity, row_count), BF16),
             pltpu.VMEM((slots, width), BF16),
             pltpu.VMEM((slots, width), BF16),
             pltpu.VMEM((slots, width), BF16),
             pltpu.VMEM((slots, width), BF16),
             pltpu.VMEM((row_count, half), BF16),
             pltpu.VMEM((row_count, half), BF16),
-            pltpu.VMEM((2 * experts - 1, row_count, piece), BF16),
+            pltpu.VMEM((experts, row_count, piece), BF16),
+            pltpu.VMEM((experts - 1, row_count, piece), BF16),
+            pltpu.VMEM((experts - 1, row_count, piece), BF16),
             pltpu.VMEM((2, plane, capacity, quarter), BF16),
             pltpu.VMEM((2, plane, capacity, quarter), BF16),
             pltpu.VMEM((2, plane, capacity, quarter), BF16),
@@ -466,7 +549,8 @@
             pltpu.VMEM((slots, units), F32),
             pltpu.VMEM((slots, 1), F32),
             pltpu.VMEM((slots, 1), F32),
-            pltpu.SemaphoreType.DMA((3,)),
+            pltpu.VMEM((row_count, width), BF16),
+            pltpu.SemaphoreType.DMA((7,)),
             pltpu.SemaphoreType.DMA((copies,)),
             pltpu.SemaphoreType.DMA((copies,)),
         ],
@@ -474,26 +558,19 @@
             collective_id=0, has_side_effects=True, vmem_limit_bytes=VMEM_MIB * 1024 * 1024
         ),
     )(
-        own_term,
-        local_cots,
-        select,
-        select.T,
+        mixer_out,
+        routes,
+        routes.T,
+        cotangent,
         resid,
         norm_gain[None],
-        router_row,
+        router.T,
         w_gate[0],
         w_up[0],
         w_down[0],
+        out_proj,
     )
     grad_down = contract_rows(activated, out_cot).astype(BF16)[None]
-    hidden = hidden_bf.astype(F32)
-    inv_rms = lax.rsqrt(jnp.mean(hidden * hidden, axis=1, keepdims=True) + 1e-05)
-    layer_out = (hidden + mixture.astype(F32)).astype(BF16)
-    hidden_cot = (
-        cotangent.astype(F32)
-        + norm_backward(hidden, inv_rms, norm_gain, normed_cot.astype(F32))
-    ).astype(BF16)
-    grad_mixer = contract_cols(hidden_cot, out_proj).astype(BF16)
     return (layer_out, grad_mixer, grad_down)
 
 

time: 122 us -> 106 us (0.87)
  matrix products: 15.5 us -> 6.77 us
  other arithmetic: 5.9 us -> 0 us
  Pallas kernels: 97.9 us -> 94.5 us
  local copies, waits for them, and re-layouts: 1.49 us -> 3.05 us
    dot_general x2 -> x0, matrix products: 7.76 us -> none  [the longest x1 3.89 us: contract_cols(): lax.dot_general(left, right, (((1,), (1,)), ((), ())), preferred_element_...]
    reduce_sum x2 -> x0, other arithmetic: 3.82 us -> none  [the longest x1 3.71 us: on_device(): jnp.mean(hidden * hidden, axis=1, keepdims=True) + 1e-05]
    pallas_call x1, Pallas kernels: 97.9 us -> 94.5 us  [on_device(): pl.pallas_call(functools.partial(layer_kernel, n_dp, experts), out_shape=...]
    unnamed x12 -> x7, local copies, waits for them, and re-layouts: 0.03 us -> 3.05 us
    transpose x1 -> x0, local copies, waits for them, and re-layouts: 1.46 us -> none  [on_device(): router_row = lax.dynamic_slice_in_dim(router, expert_id, 1, 1).T]
    convert_element_type x2 -> x0, other arithmetic: 1.33 us -> none  [on_device(): select = (hit[:, None] & (slot_pos[:, None] == jnp.arange(capacity, dtype...]
    dot_general x2 -> x1, matrix products: 7.77 us -> 6.77 us  [contract_rows(): lax.dot_general(left, right, (((0,), (0,)), ((), ())), preferred_element_...]
where the time goes in v2:
time: 106 us; the launch traced here: 105 us
  Pallas kernels  94.5 us (89%)
  matrix products  6.77 us (6%)
  local copies, waits for them, and re-layouts  3.05 us (3%)
    pallas_call x1, Pallas kernels, on_device(): pl.pallas_call(functools.partial(layer_kernel, n_dp, experts), out_shape=...  94.5 us
    dot_general x1, matrix products, contract_rows(): lax.dot_general(left, right, (((0,), (0,)), ((), ())), preferred_element_...  6.77 us
    unnamed x7, local copies, waits for them, and re-layouts  3.05 us

profile of v2, /device:TPU:0, one launch (start us, length us, event | category | flops | bytes accessed | tf_op | source)
XLA Modules:
  0.0 105.0 jit_solution(7018329807216345186)
XLA Ops:
  0.6 1.4 %copy.13.routes_ref = s32[128,2]{1,0:T(8,128)} copy(s32[128,2]{0,1:T(2,128)} %param.15) | data formatting | bytes 2048 | tf_op args[5]
  2.0 94.5 %shard_map.121 = (bf16[128,4096]{1,0:T(8,128)(2,1)}, bf16[128,512]{1,0:T(8,128)(2,1)}, bf16[192,896]{1,0:T(8,128)(2,1)}, bf16[192,4096]{1,0:T(8,128)(2,1)}) custom-call(bf16[128,512]{1,0:T(8,128)(2,1)} %mixer_ref.1, s32[128,2]{1,0:T(8,128)} %copy.13.routes_ref, s32[2,128]{1,0:T(2,128)} %bitcast.15, bf16[128,4096]{1,0:T(8,128)(2,1)} %cotangent_ref.1, ...), custom_call_target="tpu_custom_call" | custom-call | tf_op jit(solution)/shard_map/pallas_call | solution.py:510
  96.5 0.0 copy-start
  96.5 0.0 copy-start.1
  96.6 6.8 %convert_bitcast_fusion = bf16[1,896,4096]{2,1,0:T(8,128)(2,1)} fusion(bf16[192,896]{1,0:T(8,128)(2,1)} %get-tuple-element.9, bf16[192,4096]{1,0:T(8,128)(2,1)} %get-tuple-element.10), kind=kOutput, calls=%fused_computation | convolution fusion | flops 1412956160 | bytes 9256960 | tf_op jit(solution)/shard_map/dot_general | solution.py:17
  103.3 0.0 copy-done
  103.3 1.0 copy.16
  104.3 0.0 copy-done.1
  104.3 0.7 copy.17
Async XLA Ops:
  96.5 6.8 %copy-start = (bf16[128,4096]{1,0:T(8,128)(2,1)S(1)}, bf16[128,4096]{1,0:T(8,128)(2,1)}, u32[]{:S(2)}) copy-start(bf16[128,4096]{1,0:T(8,128)(2,1)} %get-tuple-element.14) | copy-start | bytes 3145732
  96.5 7.8 %copy-start.1 = (bf16[128,512]{1,0:T(8,128)(2,1)S(1)}, bf16[128,512]{1,0:T(8,128)(2,1)}, u32[]{:S(2)}) copy-start(bf16[128,512]{1,0:T(8,128)(2,1)} %get-tuple-element.15) | copy-start | bytes 393220

commit v3 on v2

--- a/solution.py
+++ b/solution.py
@@ -107,17 +107,15 @@
     return over_h, over_c
 
 
-def gather_finish(place, sender, out, over_h, over_c):
+def gather_halves(place, sender, out, over_h, over_c):
     here = place
     for d in range(here.experts):
         where = (slice(None), here.cols_e(here.step_e(-d), 1 - here.h, here.c))
         over_h[d].wait_recv()
         over_c.append(forward(here, sender, out, where, c=1 - here.c))
-    for copy in over_c:
-        copy.wait_recv()
-
-
-def gather_and_dispatch(place, sender, over_e, hidden, select_t, rows, rows_of):
+
+
+def gather_and_dispatch(place, sender, over_e, hidden, select_t, rows, rows_of, work):
     here = place
     steps_x = range(1, here.n_dp)
 
@@ -149,6 +147,7 @@
         over_h[d].wait_recv()
         over_c.append(forward(here, sender, hidden, (slice(None), other), c=1 - here.c))
         pick(other)
+    work(here.cols_h(here.h, here.c))
     for d in range(here.experts):
         cols = here.cols_e(here.step_e(-d), 1 - here.h, here.c)
         for s in steps_x:
@@ -158,7 +157,14 @@
     for copy in over_c:
         copy.wait_recv()
     pick(here.cols_c(1 - here.c))
-    return rows_c
+    early = here.experts * (here.n_dp - 1)
+    for copy in rows_c[:early]:
+        copy.wait_recv()
+    work(here.cols_h(here.h, 1 - here.c))
+    work(here.cols_h(1 - here.h, here.c))
+    for copy in rows_c[early:]:
+        copy.wait_recv()
+    work(here.cols_h(1 - here.h, 1 - here.c))
 
 
 def tiles(extent, most):
@@ -172,7 +178,6 @@
     n_dp,
     experts,
     mixer_ref,
-    routes_ref,
     routes_t,
     cotangent_ref,
     resid_ref,
@@ -217,7 +222,14 @@
     pre_up,
     gates,
     slopes,
-    hidden_cot,
+    squares,
+    logits,
+    weighted,
+    inv_rows,
+    inner,
+    cot_proj,
+    hidden_proj,
+    change_proj,
     load_sems,
     send_sems,
     recv_sems,
@@ -253,10 +265,10 @@
     ]
     greet(devices)
 
-    hit = ((routes_ref[:, 0:1] == here.e) | (routes_ref[:, 1:2] == here.e)).astype(F32)
     hit_t = ((routes_t[0:1, :] == here.e) | (routes_t[1:2, :] == here.e)).astype(F32)
     row = lax.broadcasted_iota(jnp.int32, (row_count, row_count), 0)
     col = lax.broadcasted_iota(jnp.int32, (row_count, row_count), 1)
+    hit = jnp.sum(jnp.where(row == col, hit_t, 0.0), axis=1, keepdims=True)
     slot = jnp.sum(jnp.where(col < row, hit_t, 0.0), axis=1, keepdims=True)
     slot_t = jnp.sum(jnp.where(row < col, hit, 0.0), axis=0, keepdims=True)
     number = lax.broadcasted_iota(jnp.int32, (row_count, capacity), 1).astype(F32)
@@ -343,43 +355,38 @@
         raw_cot[...] += contract_cols(slot_cot[:, cols], w_down[:, cols])
 
     router_row = router_ref.at[pl.ds(here.e, 1), :]
-    rows_c = gather_and_dispatch(here, sender, over_e, hidden, select_t, rows, rows_of)
-
-    def norm_rows(x):
-        @pl.loop(0, capacity // 16)
-        def _(k):
-            block = pl.ds(pl.multiple_of(x * capacity + k * 16, 16), 16)
-            value = rows[block, :].astype(F32)
-            inv_rms = lax.rsqrt(jnp.mean(value * value, axis=1, keepdims=True) + 1e-05)
-            normed = (value * inv_rms * gain_ref[...]).astype(BF16)
-            own_in[block, :] = normed
-            logit = jnp.sum(normed.astype(F32) * router_row[...], axis=1, keepdims=True)
-            gate = jax.nn.sigmoid(logit)
-            gates[block, :] = gate
-            out_cot_ref[block, :] = (gate * slot_cot[block, :].astype(F32)).astype(BF16)
-
-    norm_rows(here.x)
-    for copy in rows_c:
-        copy.wait_recv()
-    for d in range(1, n_dp):
-        norm_rows(here.step_x(d))
-
+
+    for ref in (pre_gate, pre_up, squares, logits):
+        ref[...] = jnp.zeros_like(ref)
     loads[1].wait()
     loads[2].wait()
-    pre_gate[...] = jnp.zeros_like(pre_gate)
-    pre_up[...] = jnp.zeros_like(pre_up)
-
-    @pl.loop(0, steps)
-    def _(k):
-        cols = pl.ds(pl.multiple_of(k * depth, depth), depth)
+
+    def expert_columns(cols):
+        @pl.loop(0, slots // 16)
+        def _(k):
+            block = pl.ds(pl.multiple_of(k * 16, 16), 16)
+            value = rows[block, cols].astype(F32)
+            scaled = (value * gain_ref[:, cols]).astype(BF16)
+            own_in[block, cols] = scaled
+            squares[block, :] += jnp.sum(value * value, axis=1, keepdims=True)
+            logits[block, :] += jnp.sum(
+                scaled.astype(F32) * router_row[:, cols], axis=1, keepdims=True
+            )
+
         pre_gate[...] += jnp.dot(own_in[:, cols], w_gate[cols, :], preferred_element_type=F32)
         pre_up[...] += jnp.dot(own_in[:, cols], w_up[cols, :], preferred_element_type=F32)
+
+    gather_and_dispatch(
+        here, sender, over_e, hidden, select_t, rows, rows_of, expert_columns
+    )
+    squares[...] = lax.rsqrt(squares[...] / width + 1e-05)
+    gates[...] = jax.nn.sigmoid(logits[...] * squares[...])
 
     @pl.loop(0, slots // 16)
     def _(k):
         block = pl.ds(pl.multiple_of(k * 16, 16), 16)
-        gate, raw = gates[block, :], raw_cot[block, :]
-        z, up = pre_gate[block, :], pre_up[block, :]
+        gate, raw, inv_rms = gates[block, :], raw_cot[block, :], squares[block, :]
+        z, up = pre_gate[block, :] * inv_rms, pre_up[block, :] * inv_rms
         sig = jax.nn.sigmoid(z)
         act = (z * sig * up).astype(BF16)
         act_ref[block, :] = act
@@ -438,6 +445,22 @@
                         crossing[i, k] = sender.start(
                             paired.at[i, k], parts.at[i, k], here.device(x=here.step_x(d), h=h)
                         )
+
+    @pl.loop(0, slots // 16)
+    def _(k):
+        block = pl.ds(pl.multiple_of(k * 16, 16), 16)
+        out_cot_ref[block, :] = (gates[block, :] * slot_cot[block, :].astype(F32)).astype(BF16)
+
+    @pl.loop(0, row_count // 16)
+    def _(k):
+        block = pl.ds(pl.multiple_of(k * 16, 16), 16)
+        value = hidden[block, :].astype(F32)
+        inv_rows[block, :] = lax.rsqrt(jnp.mean(value * value, axis=1, keepdims=True) + 1e-05)
+
+    cot_proj[...] = contract_cols(cotangent_ref[...], w_proj[...])
+    hidden_proj[...] = contract_cols(hidden[...], w_proj[...])
+    inner[...] = jnp.zeros_like(inner)
+    change_proj[...] = jnp.zeros_like(change_proj)
 
     own_slot = plane.index((0, 0))
     mine_cols = pl.ds(pl.multiple_of(here.e * here.piece, here.piece), here.piece)
@@ -467,7 +490,9 @@
         result[:, own_cols] = total.astype(BF16)
         started.append(gather_start(here, sender, result))
     cot_passed = gather_pass(here, sender, cot, started[1])
-    gather_finish(here, sender, mix, *mix_passed)
+    gather_halves(here, sender, mix, *mix_passed)
+    for copy in mix_passed[1]:
+        copy.wait_recv()
 
     @pl.loop(0, row_count // 16)
     def _(k):
@@ -476,20 +501,40 @@
             BF16
         )
 
-    gather_finish(here, sender, cot, *cot_passed)
-
-    @pl.loop(0, row_count // 16)
-    def _(k):
-        block = pl.ds(pl.multiple_of(k * 16, 16), 16)
-        value = hidden[block, :].astype(F32)
-        inv_rms = lax.rsqrt(jnp.mean(value * value, axis=1, keepdims=True) + 1e-05)
-        weighted = cot[block, :].astype(F32) * gain_ref[...]
-        inner_mean = jnp.mean(weighted * value, axis=1, keepdims=True)
-        change = inv_rms * weighted - inv_rms * inv_rms * inv_rms * value * inner_mean
-        hidden_cot[block, :] = (cotangent_ref[block, :].astype(F32) + change).astype(BF16)
-
-    mixer_cot_ref[...] = contract_cols(hidden_cot[...], w_proj[...]).astype(BF16)
+    def change_columns(cols):
+        @pl.loop(0, row_count // 16)
+        def _(k):
+            block = pl.ds(pl.multiple_of(k * 16, 16), 16)
+            scaled = cot[block, cols].astype(F32) * gain_ref[:, cols]
+            weighted[block, cols] = scaled.astype(BF16)
+            inner[block, :] += jnp.sum(
+                scaled * hidden[block, cols].astype(F32), axis=1, keepdims=True
+            )
+
+        change_proj[...] += contract_cols(weighted[:, cols], w_proj[:, cols])
+
+    gather_halves(here, sender, cot, *cot_passed)
+    change_columns(here.cols_h(here.h, here.c))
+    from_core = cot_passed[1]
+    for copy in from_core[:experts]:
+        copy.wait_recv()
+    change_columns(here.cols_h(here.h, 1 - here.c))
+    change_columns(here.cols_h(1 - here.h, here.c))
+    for copy in from_core[experts:]:
+        copy.wait_recv()
+    change_columns(here.cols_h(1 - here.h, 1 - here.c))
+    inv_rms = inv_rows[...]
+    along = inv_rms * inv_rms * inv_rms * (inner[...] / width)
+    mixer_cot_ref[...] = (
+        cot_proj[...] + inv_rms * change_proj[...] - along * hidden_proj[...]
+    ).astype(BF16)
     sender.finish()
+
+
+def result_kernel(act_ref, out_cot_ref, layer_ref, mixer_cot_ref, down_ref, layer_out, mixer_out):
+    down_ref[...] = contract_rows(act_ref[...], out_cot_ref[...]).astype(BF16)
+    layer_out[...] = layer_ref[...]
+    mixer_out[...] = mixer_cot_ref[...]
 
 
 def on_device(
@@ -515,7 +560,7 @@
             jax.ShapeDtypeStruct((slots, units), BF16),
             jax.ShapeDtypeStruct((slots, width), BF16),
         ],
-        in_specs=[whole] * 7 + [remote] * 4,
+        in_specs=[whole] * 6 + [remote] * 4,
         out_specs=[whole] * 4,
         scratch_shapes=[
             pltpu.VMEM((width, units), BF16),
@@ -549,7 +594,14 @@
             pltpu.VMEM((slots, units), F32),
             pltpu.VMEM((slots, 1), F32),
             pltpu.VMEM((slots, 1), F32),
+            pltpu.VMEM((slots, 1), F32),
+            pltpu.VMEM((slots, 1), F32),
             pltpu.VMEM((row_count, width), BF16),
+            pltpu.VMEM((row_count, 1), F32),
+            pltpu.VMEM((row_count, 1), F32),
+            pltpu.VMEM(mixer_out.shape, F32),
+            pltpu.VMEM(mixer_out.shape, F32),
+            pltpu.VMEM(mixer_out.shape, F32),
             pltpu.SemaphoreType.DMA((7,)),
             pltpu.SemaphoreType.DMA((copies,)),
             pltpu.SemaphoreType.DMA((copies,)),
@@ -559,7 +611,6 @@
         ),
     )(
         mixer_out,
-        routes,
         routes.T,
         cotangent,
         resid,
@@ -570,7 +621,29 @@
         w_down[0],
         out_proj,
     )
-    grad_down = contract_rows(activated, out_cot).astype(BF16)[None]
+    span, spans = tiles(width, 1024)
+    grad_down, layer_out, grad_mixer = pl.pallas_call(
+        result_kernel,
+        grid=(spans,),
+        out_shape=[
+            jax.ShapeDtypeStruct((units, width), BF16),
+            jax.ShapeDtypeStruct((row_count, width), BF16),
+            jax.ShapeDtypeStruct(mixer_out.shape, BF16),
+        ],
+        in_specs=[
+            pl.BlockSpec((slots, units), lambda j: (0, 0)),
+            pl.BlockSpec((slots, span), lambda j: (0, j)),
+            pl.BlockSpec((row_count, span), lambda j: (0, j)),
+            pl.BlockSpec(mixer_out.shape, lambda j: (0, 0)),
+        ],
+        out_specs=[
+            pl.BlockSpec((units, span), lambda j: (0, j)),
+            pl.BlockSpec((row_count, span), lambda j: (0, j)),
+            pl.BlockSpec(mixer_out.shape, lambda j: (0, 0)),
+        ],
+        compiler_params=pltpu.CompilerParams(vmem_limit_bytes=32 * 1024 * 1024),
+    )(activated, out_cot, layer_out, grad_mixer)
+    grad_down = grad_down[None]
     return (layer_out, grad_mixer, grad_down)
 
 

time: 106 us -> 108 us (1.019)
  Pallas kernels: 94.5 us -> 102 us
  matrix products: 6.77 us -> 0 us
  local copies, waits for them, and re-layouts: 3.05 us -> 4.51 us
    dot_general x1 -> x0, matrix products: 6.77 us -> none  [contract_rows(): lax.dot_general(left, right, (((0,), (0,)), ((), ())), preferred_element_...]
    pallas_call x0 -> x1, Pallas kernels: none -> 4.75 us  [on_device(): pl.pallas_call(result_kernel, grid=(spans,), out_shape=[jax.ShapeDtypeStr...]
    pallas_call x1, Pallas kernels: 94.5 us -> 97.4 us  [on_device(): pl.pallas_call(functools.partial(layer_kernel, n_dp, experts), out_shape=...]
    unnamed x7 -> x8, local copies, waits for them, and re-layouts: 3.05 us -> 4.51 us
where the time goes in v3:
time: 108 us; the launch traced here: 107 us
  Pallas kernels  102 us (94%)
  local copies, waits for them, and re-layouts  4.51 us (4%)
    pallas_call x1, Pallas kernels, on_device(): pl.pallas_call(functools.partial(layer_kernel, n_dp, experts), out_shape=...  97.4 us
    pallas_call x1, Pallas kernels, on_device(): pl.pallas_call(result_kernel, grid=(spans,), out_shape=[jax.ShapeDtypeStr...  4.75 us
    unnamed x8, local copies, waits for them, and re-layouts  4.51 us

profile of v3, /device:TPU:0, one launch (start us, length us, event | category | flops | bytes accessed | tf_op | source)
XLA Modules:
  0.0 107.4 jit_solution(9678096721170800120)
XLA Ops:
  0.6 97.4 %shard_map.121 = (bf16[128,4096]{1,0:T(8,128)(2,1)}, bf16[128,512]{1,0:T(8,128)(2,1)}, bf16[192,896]{1,0:T(8,128)(2,1)}, bf16[192,4096]{1,0:T(8,128)(2,1)}) custom-call(bf16[128,512]{1,0:T(8,128)(2,1)} %mixer_ref.1, s32[2,128]{1,0:T(2,128)} %bitcast.12, bf16[128,4096]{1,0:T(8,128)(2,1)} %cotangent_ref.1, bf16[128,4096]{1,0:T(8,128)(2,1)} %resid_ref.1, ...), custom_call_target="tpu_custom_call" | custom-call | tf_op jit(solution)/shard_map/pallas_call | solution.py:555
  98.1 0.0 copy-start
  98.1 1.4 %copy-done = bf16[192,4096]{1,0:T(8,128)(2,1)S(1)} copy-done((bf16[192,4096]{1,0:T(8,128)(2,1)S(1)}, bf16[192,4096]{1,0:T(8,128)(2,1)}, u32[]{:S(2)}) %copy-start) | copy-done | bytes 1572888
  99.5 0.0 copy-start.1
  99.5 1.2 %copy-done.1 = bf16[128,4096]{1,0:T(8,128)(2,1)S(1)} copy-done((bf16[128,4096]{1,0:T(8,128)(2,1)S(1)}, bf16[128,4096]{1,0:T(8,128)(2,1)}, u32[]{:S(2)}) %copy-start.1) | copy-done | bytes 1048600
  100.7 0.0 copy-start.2
  100.7 1.0 copy-done.2
  101.7 0.0 copy-start.3
  101.7 0.9 copy-done.3
  102.6 4.8 %shard_map.122 = (bf16[896,4096]{1,0:T(8,128)(2,1)}, bf16[128,4096]{1,0:T(8,128)(2,1)}, bf16[128,512]{1,0:T(8,128)(2,1)}) custom-call(bf16[192,896]{1,0:T(8,128)(2,1)S(1)} %copy-done.2, bf16[192,4096]{1,0:T(8,128)(2,1)S(1)} %copy-done, bf16[128,4096]{1,0:T(8,128)(2,1)S(1)} %copy-done.1, bf16[128,512]{1,0:T(8,128)(2,1)S(1)} %copy-done.3), custom_call_target="tpu_custom_call" | custom-call | tf_op jit(solution)/shard_map/pallas_call | solution.py:625
Async XLA Ops:
  98.1 1.4 %copy-start = (bf16[192,4096]{1,0:T(8,128)(2,1)S(1)}, bf16[192,4096]{1,0:T(8,128)(2,1)}, u32[]{:S(2)}) copy-start(bf16[192,4096]{1,0:T(8,128)(2,1)} %get-tuple-element.11.out_cot_ref) | copy-start | bytes 4718596
  99.5 1.2 %copy-start.1 = (bf16[128,4096]{1,0:T(8,128)(2,1)S(1)}, bf16[128,4096]{1,0:T(8,128)(2,1)}, u32[]{:S(2)}) copy-start(bf16[128,4096]{1,0:T(8,128)(2,1)} %get-tuple-element.12.layer_ref) | copy-start | bytes 3145732
  100.7 1.0 copy-start.2
  101.7 0.9 copy-start.3

commit v4 on v2

--- a/solution.py
+++ b/solution.py
@@ -172,7 +172,6 @@
     n_dp,
     experts,
     mixer_ref,
-    routes_ref,
     routes_t,
     cotangent_ref,
     resid_ref,
@@ -218,6 +217,7 @@
     gates,
     slopes,
     hidden_cot,
+    inv_rows,
     load_sems,
     send_sems,
     recv_sems,
@@ -253,10 +253,10 @@
     ]
     greet(devices)
 
-    hit = ((routes_ref[:, 0:1] == here.e) | (routes_ref[:, 1:2] == here.e)).astype(F32)
     hit_t = ((routes_t[0:1, :] == here.e) | (routes_t[1:2, :] == here.e)).astype(F32)
     row = lax.broadcasted_iota(jnp.int32, (row_count, row_count), 0)
     col = lax.broadcasted_iota(jnp.int32, (row_count, row_count), 1)
+    hit = jnp.sum(jnp.where(row == col, hit_t, 0.0), axis=1, keepdims=True)
     slot = jnp.sum(jnp.where(col < row, hit_t, 0.0), axis=1, keepdims=True)
     slot_t = jnp.sum(jnp.where(row < col, hit, 0.0), axis=0, keepdims=True)
     number = lax.broadcasted_iota(jnp.int32, (row_count, capacity), 1).astype(F32)
@@ -356,7 +356,6 @@
             logit = jnp.sum(normed.astype(F32) * router_row[...], axis=1, keepdims=True)
             gate = jax.nn.sigmoid(logit)
             gates[block, :] = gate
-            out_cot_ref[block, :] = (gate * slot_cot[block, :].astype(F32)).astype(BF16)
 
     norm_rows(here.x)
     for copy in rows_c:
@@ -438,6 +437,17 @@
                         crossing[i, k] = sender.start(
                             paired.at[i, k], parts.at[i, k], here.device(x=here.step_x(d), h=h)
                         )
+
+    @pl.loop(0, slots // 16)
+    def _(k):
+        block = pl.ds(pl.multiple_of(k * 16, 16), 16)
+        out_cot_ref[block, :] = (gates[block, :] * slot_cot[block, :].astype(F32)).astype(BF16)
+
+    @pl.loop(0, row_count // 16)
+    def _(k):
+        block = pl.ds(pl.multiple_of(k * 16, 16), 16)
+        value = hidden[block, :].astype(F32)
+        inv_rows[block, :] = lax.rsqrt(jnp.mean(value * value, axis=1, keepdims=True) + 1e-05)
 
     own_slot = plane.index((0, 0))
     mine_cols = pl.ds(pl.multiple_of(here.e * here.piece, here.piece), here.piece)
@@ -482,7 +492,7 @@
     def _(k):
         block = pl.ds(pl.multiple_of(k * 16, 16), 16)
         value = hidden[block, :].astype(F32)
-        inv_rms = lax.rsqrt(jnp.mean(value * value, axis=1, keepdims=True) + 1e-05)
+        inv_rms = inv_rows[block, :]
         weighted = cot[block, :].astype(F32) * gain_ref[...]
         inner_mean = jnp.mean(weighted * value, axis=1, keepdims=True)
         change = inv_rms * weighted - inv_rms * inv_rms * inv_rms * value * inner_mean
@@ -490,6 +500,12 @@
 
     mixer_cot_ref[...] = contract_cols(hidden_cot[...], w_proj[...]).astype(BF16)
     sender.finish()
+
+
+def result_kernel(act_ref, out_cot_ref, layer_ref, mixer_cot_ref, down_ref, layer_out, mixer_out):
+    down_ref[...] = contract_rows(act_ref[...], out_cot_ref[...]).astype(BF16)
+    layer_out[...] = layer_ref[...]
+    mixer_out[...] = mixer_cot_ref[...]
 
 
 def on_device(
@@ -515,7 +531,7 @@
             jax.ShapeDtypeStruct((slots, units), BF16),
             jax.ShapeDtypeStruct((slots, width), BF16),
         ],
-        in_specs=[whole] * 7 + [remote] * 4,
+        in_specs=[whole] * 6 + [remote] * 4,
         out_specs=[whole] * 4,
         scratch_shapes=[
             pltpu.VMEM((width, units), BF16),
@@ -550,6 +566,7 @@
             pltpu.VMEM((slots, 1), F32),
             pltpu.VMEM((slots, 1), F32),
             pltpu.VMEM((row_count, width), BF16),
+            pltpu.VMEM((row_count, 1), F32),
             pltpu.SemaphoreType.DMA((7,)),
             pltpu.SemaphoreType.DMA((copies,)),
             pltpu.SemaphoreType.DMA((copies,)),
@@ -559,7 +576,6 @@
         ),
     )(
         mixer_out,
-        routes,
         routes.T,
         cotangent,
         resid,
@@ -570,7 +586,29 @@
         w_down[0],
         out_proj,
     )
-    grad_down = contract_rows(activated, out_cot).astype(BF16)[None]
+    span, spans = tiles(width, 1024)
+    grad_down, layer_out, grad_mixer = pl.pallas_call(
+        result_kernel,
+        grid=(spans,),
+        out_shape=[
+            jax.ShapeDtypeStruct((units, width), BF16),
+            jax.ShapeDtypeStruct((row_count, width), BF16),
+            jax.ShapeDtypeStruct(mixer_out.shape, BF16),
+        ],
+        in_specs=[
+            pl.BlockSpec((slots, units), lambda j: (0, 0)),
+            pl.BlockSpec((slots, span), lambda j: (0, j)),
+            pl.BlockSpec((row_count, span), lambda j: (0, j)),
+            pl.BlockSpec(mixer_out.shape, lambda j: (0, 0)),
+        ],
+        out_specs=[
+            pl.BlockSpec((units, span), lambda j: (0, j)),
+            pl.BlockSpec((row_count, span), lambda j: (0, j)),
+            pl.BlockSpec(mixer_out.shape, lambda j: (0, 0)),
+        ],
+        compiler_params=pltpu.CompilerParams(vmem_limit_bytes=VMEM_MIB * 1024 * 1024),
+    )(activated, out_cot, layer_out, grad_mixer)
+    grad_down = grad_down[None]
     return (layer_out, grad_mixer, grad_down)
 
 

time: 106 us -> 102 us (0.962)
  matrix products: 6.77 us -> 0 us
  Pallas kernels: 94.5 us -> 99.5 us
  local copies, waits for them, and re-layouts: 3.05 us -> 0 us
    dot_general x1 -> x0, matrix products: 6.77 us -> none  [contract_rows(): lax.dot_general(left, right, (((0,), (0,)), ((), ())), preferred_element_...]
    pallas_call x0 -> x1, Pallas kernels: none -> 6.62 us  [on_device(): pl.pallas_call(result_kernel, grid=(spans,), out_shape=[jax.ShapeDtypeStr...]
    unnamed x7 -> x0, local copies, waits for them, and re-layouts: 3.05 us -> none
    pallas_call x1, Pallas kernels: 94.5 us -> 92.9 us  [on_device(): pl.pallas_call(functools.partial(layer_kernel, n_dp, experts), out_shape=...]
where the time goes in v4:
time: 102 us; the launch traced here: 100 us
  Pallas kernels  99.5 us (98%)
    pallas_call x1, Pallas kernels, on_device(): pl.pallas_call(functools.partial(layer_kernel, n_dp, experts), out_shape=...  92.9 us
    pallas_call x1, Pallas kernels, on_device(): pl.pallas_call(result_kernel, grid=(spans,), out_shape=[jax.ShapeDtypeStr...  6.62 us

profile of v4, /device:TPU:0, one launch (start us, length us, event | category | flops | bytes accessed | tf_op | source)
XLA Modules:
  0.0 100.2 jit_solution(4659589479655355747)
XLA Ops:
  0.6 92.9 %shard_map.121 = (bf16[128,4096]{1,0:T(8,128)(2,1)}, bf16[128,512]{1,0:T(8,128)(2,1)}, bf16[192,896]{1,0:T(8,128)(2,1)}, bf16[192,4096]{1,0:T(8,128)(2,1)}) custom-call(bf16[128,512]{1,0:T(8,128)(2,1)} %mixer_ref.1, s32[2,128]{1,0:T(2,128)} %bitcast.12, bf16[128,4096]{1,0:T(8,128)(2,1)} %cotangent_ref.1, bf16[128,4096]{1,0:T(8,128)(2,1)} %resid_ref.1, ...), custom_call_target="tpu_custom_call" | custom-call | tf_op jit(solution)/shard_map/pallas_call | solution.py:526
  93.6 6.6 %shard_map.122 = (bf16[896,4096]{1,0:T(8,128)(2,1)}, bf16[128,4096]{1,0:T(8,128)(2,1)}, bf16[128,512]{1,0:T(8,128)(2,1)}) custom-call(bf16[192,896]{1,0:T(8,128)(2,1)} %get-tuple-element.10.act_ref, bf16[192,4096]{1,0:T(8,128)(2,1)} %get-tuple-element.11.out_cot_ref, bf16[128,4096]{1,0:T(8,128)(2,1)} %get-tuple-element.12.layer_ref, ...), custom_call_target="tpu_custom_call" | custom-call | tf_op jit(solution)/shard_map/pallas_call | solution.py:590
